TPU v7x, 256 devices: a whole 4x4x8 slice. The times are simulated.
256 devices in a mesh: owner: 32 (over y, z_hi, x), group: 8 (over z_lo, core).
Axes of the slice: x: 4, y: 4, z: 8 (z_hi: 2, z_lo: 4; z = z_hi * 4 + z_lo), core: 2. Of those that a mesh axis runs over, the one named last changes fastest.
Arguments:
- queries: bfloat16 [128, 8192], P('group', 'owner'), may hold values from -110 to 110
- keys: bfloat16 [4, 32768, 1024], P(None, ('owner', 'group')), may hold values from -5 to 5
- values: bfloat16 [4, 32768, 1024], P(None, ('owner', 'group')), may hold values from -6 to 6
- req_doc: int32 [128, 1], replicated, may hold values from 0 to 3; in each aligned block of 16 rows (0 to 15, 16 to 31, ...) at most 8 rows name the same one
Outputs:
- attended: bfloat16 [128, 8192], P('group', 'owner')
Inputs may be any that keep to these rules, and one draw needn't show every extreme that they name: `req_doc`: among the 16 requests of one group no document is read by more than 8 requests, a bound that some block reaches.
All inputs are finite; a program needn't handle non-finite values.
Results may differ from a plain program's by a relative error of at most 0.0021.
Values may be sent and summed in bfloat16 or wider, within the bound.
No kernel may reach another device: no remote copies, remote signals or barrier semaphores. Data moves between devices by JAX's collectives and lax.ppermute only.
A program may use at most 64 MiB of HBM per device.

v0:
```python
import math

import jax
import jax.numpy as jnp
from jax import lax
from jax.sharding import PartitionSpec as P

HQ = 64
KV = 8
HD = 128
GQ = 8
SLOTS = 8


def body(queries, keys, values, req_doc):
    n_owner = lax.axis_size("owner")
    n_group = lax.axis_size("group")
    rows_group = queries.shape[0]
    doc_count, tok_dev, kv_width = keys.shape
    heads_dev = HQ // n_owner
    by_groups = lax.all_gather(queries, "group", axis=0, tiled=True)
    gathered = lax.all_gather(by_groups, "owner", axis=1, tiled=True)
    total_rows = gathered.shape[0]
    doc_ids = req_doc[:, 0]
    onehot = (doc_ids[:, None] == jnp.arange(doc_count, dtype=jnp.int32)[None, :]).astype(jnp.int32)
    grouped = onehot.reshape(n_group, rows_group, doc_count)
    ranking = (jnp.cumsum(grouped, axis=1) - grouped).reshape(total_rows, doc_count)
    group_of = jnp.arange(total_rows, dtype=jnp.int32) // rows_group
    target = group_of[:, None] * SLOTS + ranking
    slot_ids = jnp.arange(n_group * SLOTS, dtype=jnp.int32)
    select = (onehot.T[:, None, :] == 1) & (target.T[:, None, :] == slot_ids[None, :, None])
    sel_float = select.astype(jnp.float32)
    slot_rows = n_group * SLOTS
    picked = jnp.einsum(
        "dsr,rf->dsf", select.astype(jnp.bfloat16), gathered, preferred_element_type=jnp.float32
    ).astype(jnp.bfloat16)
    numer = jnp.zeros((total_rows, HQ * HD), jnp.float32)
    maxima = jnp.zeros((total_rows, HQ), jnp.float32)
    sums = jnp.zeros((total_rows, HQ), jnp.float32)
    for doc_index in range(doc_count):
        rows_q = picked[doc_index].reshape(slot_rows, KV, GQ, HD)
        key_stretch = keys[doc_index].reshape(tok_dev, KV, HD)
        value_stretch = values[doc_index].reshape(tok_dev, KV, HD)
        scores = jnp.einsum(
            "rkgh,tkh->rkgt", rows_q, key_stretch, preferred_element_type=jnp.float32
        ) / math.sqrt(HD)
        block_top = jnp.max(scores, axis=-1)
        expo = jnp.exp(scores - block_top[..., None])
        block_sum = jnp.sum(expo, axis=-1)
        weights = expo.astype(jnp.bfloat16)
        block_out = jnp.einsum(
            "rkgt,tkh->rkgh", weights, value_stretch, preferred_element_type=jnp.float32
        )
        chooser = sel_float[doc_index]
        numer = numer + jnp.einsum(
            "sr,sf->rf",
            chooser,
            block_out.reshape(slot_rows, HQ * HD),
            precision=lax.Precision.HIGHEST,
        )
        maxima = maxima + jnp.einsum(
            "sr,sf->rf", chooser, block_top.reshape(slot_rows, HQ), precision=lax.Precision.HIGHEST
        )
        sums = sums + jnp.einsum(
            "sr,sf->rf", chooser, block_sum.reshape(slot_rows, HQ), precision=lax.Precision.HIGHEST
        )
    top_all = lax.pmax(maxima.astype(jnp.bfloat16), ("owner", "group")).astype(maxima.dtype)
    factor = jnp.exp(maxima - top_all)
    scaled = (numer.reshape(total_rows, HQ, HD) * factor[..., None]).reshape(total_rows, HQ * HD)
    weighted = sums * factor
    part_num, part_den = (
        lax.psum_scatter(scaled, "owner", scatter_dimension=1, tiled=True),
        lax.psum_scatter(weighted, "owner", scatter_dimension=1, tiled=True),
    )
    mine_num, mine_den = (
        lax.psum_scatter(part_num, "group", scatter_dimension=0, tiled=True),
        lax.psum_scatter(part_den, "group", scatter_dimension=0, tiled=True),
    )
    result = mine_num.reshape(rows_group, heads_dev, HD) / mine_den[..., None]
    result = result.reshape(rows_group, heads_dev * HD).astype(jnp.bfloat16)
    return result


def solution(mesh):
    placed = (
        P("group", "owner"),
        P(None, ("owner", "group"), None),
        P(None, ("owner", "group"), None),
        P(),
    )
    return jax.shard_map(
        body, mesh=mesh, in_specs=placed, out_specs=P("group", "owner"), check_vma=False
    )
```

profile of v0, /device:TPU:8, one launch (start us, length us, event | category | flops | bytes accessed | tf_op | source)
XLA Modules:
  0.0 553.2 jit_solution(6543874578296809337)
XLA Ops:
  6.5 16.1 %all_gather.6 = bf16[128,256]{1,0:T(8,128)(2,1)} all-gather(bf16[16,256]{1,0:T(8,128)(2,1)} %param.4), channel_id=1, replica_groups=mesh['owner'=32,'group'=8] {'group'}, dimensions={0}, use_global_device_ids=true | all-gather | bytes 73728 | tf_op jit(solution)/shard_map/all_gather | solution.py:21
  30.6 91.4 %all-gather.2.cloned.1.call-done = bf16[128,8192]{1,0:T(8,128)(2,1)} async-done(((bf16[128,256]{1,0:T(8,128)(2,1)}), bf16[128,8192]{1,0:T(8,128)(2,1)}) %all-gather.2.cloned.1.call-update) | async-done | bytes 2097168 | tf_op jit(solution)/shard_map/all_gather | solution.py:22
  122.1 2.8 convolution_convert_fusion
  130.4 1.9 convolution_bitcast_fusion.3
  132.3 1.6 copy.51
  133.9 2.0 bitcast_reduce_fusion.2
  136.0 2.2 convolution_bitcast_fusion.2
  138.3 1.6 copy.57
  139.9 2.0 bitcast_reduce_fusion.1
  142.0 2.2 convolution_bitcast_fusion.1
  144.2 1.6 copy.63
  145.8 2.0 bitcast_reduce_fusion
  148.6 72.6 %pmax.7 = bf16[128,64]{0,1:T(8,128)(2,1)S(1)} all-reduce(bf16[128,64]{0,1:T(8,128)(2,1)S(1)} %get-tuple-element.25), channel_id=1, replica_groups=mesh['owner'=32,'group'=8] {'owner','group'}, use_global_device_ids=true, to_apply=%region_5.6 | all-reduce | flops 8192 | bytes 32768 | tf_op jit(solution)/shard_map/pmax | solution.py:67
  221.3 2.4 convolution_bitcast_fusion
  225.3 3.1 fusion.7
  228.5 3.4 convolution_add_fusion.2
  231.9 3.4 convolution_add_fusion.1
  236.5 7.8 %fusion = f32[128,8192]{1,0:T(8,128)} fusion(f32[128,8192]{1,0:T(8,128)S(1)} %convolution_add_fusion.1, f32[16,8,64,128]{3,2,1,0:T(8,128)S(1)} %bitcast.203, f32[8,8,64,128]{3,2,1,0:T(8,128)S(1)} %bitcast.204, pred[4,64,128]{2,1,0:T(32,128)(4,1)S(1)} %fusion.44), kind=kOutput, calls=%fused_computation.2 | convolution fusion | flops 807403520 | bytes 14688256 | tf_op jit(solution)/shard_map/sr,sf->rf/dot_general | solution.py:55
  247.6 2.6 fusion.17
  251.8 2.5 fusion.21
  255.1 201.9 %all-reduce = f32[128,64]{0,1:T(8,128)S(1)} all-reduce(f32[128,64]{0,1:T(8,128)S(1)} %fusion.23), channel_id=4, replica_groups=mesh['owner'=32,'group'=8] {'owner'}, use_global_device_ids=true, to_apply=%region_12.13.clone | all-reduce | flops 8192 | bytes 65536
  457.8 3.4 reduce-scatter.6.cloned.1.call-done
  461.2 46.9 %reduce-scatter.10.cloned.1.call-done = f32[16,2]{1,0:T(8,128)} async-done(((f32[128,2]{1,0:T(8,128)}), f32[16,2]{1,0:T(8,128)}) %reduce-scatter.10.cloned.1.call-update) | async-done | bytes 144 | tf_op jit(solution)/shard_map/reduce_scatter | solution.py:77
  508.1 36.5 %reduce-scatter.8.cloned.1.call-done = f32[16,256]{1,0:T(8,128)} async-done(((f32[128,256]{1,0:T(8,128)}), f32[16,256]{1,0:T(8,128)}) %reduce-scatter.8.cloned.1.call-update) | async-done | bytes 16400 | tf_op jit(solution)/shard_map/reduce_scatter | solution.py:76
  (82 shorter events, 25.1 us)
Async XLA Ops:
  6.5 115.5 %all-gather.2.cloned.1.call-start = ((), (), s32[]{:S(2)}) async-start(), calls=%async_computation.3 | async-start | bytes 2162688 | tf_op jit(solution)/shard_map/all_gather | solution.py:22
  22.6 438.6 %reduce-scatter.6.cloned.1.call-start = ((), (), s32[]{:S(2)}) async-start(), calls=%async_computation.4 | async-start | bytes 4325376 | tf_op jit(solution)/shard_map/reduce_scatter | solution.py:72
  25.0 2.1 copy-start.7
  27.0 3.5 copy-start.8
  132.3 1.6 copy-start.6
  138.3 1.6 copy-start.5
  144.2 1.6 copy-start.4
  223.7 1.6 copy-start.1
  225.3 3.2 copy-start.2
  228.5 3.4 copy-start.3
  244.3 0.7 copy-start.9
  244.3 263.8 %reduce-scatter.10.cloned.1.call-start = ((), (), s32[]{:S(2)}) async-start(), calls=%async_computation.6 | async-start | bytes 73728 | tf_op jit(solution)/shard_map/reduce_scatter | solution.py:77
  247.5 2.9 copy-start
  457.8 86.8 %reduce-scatter.8.cloned.1.call-start = ((), (), s32[]{:S(2)}) async-start(), calls=%async_computation.5 | async-start | bytes 147456 | tf_op jit(solution)/shard_map/reduce_scatter | solution.py:76
Sparse Core Ops, SparseCore 0:
  22.7 99.2 all-gather.1
  244.4 216.7 reduce-scatter.5
  463.7 44.3 reduce-scatter.9
  510.6 33.9 reduce-scatter.7
where the time goes:
time: 554 us; the launch traced here: 553 us
  blocking collectives  291 us (53%)
  waiting for transfers between devices  178 us (32%)
  matrix products  37.4 us (7%)
  local copies, waits for them, and re-layouts  22.2 us (4%)
  between operations  14.1 us (3%)
  other arithmetic  10.6 us (2%)
    unnamed x1, blocking collectives  202 us
    all_gather x1, waiting for transfers between devices, body(): gathered = lax.all_gather(by_groups, 'owner', axis=1, tiled=True)  91.4 us
    pmax x1, blocking collectives, body(): lax.pmax(maxima.astype(jnp.bfloat16), ('owner', 'group'))  72.6 us
    reduce_scatter x1, waiting for transfers between devices, body(): lax.psum_scatter(part_den, 'group', scatter_dimension=0, tiled=True)  46.9 us
    reduce_scatter x1, waiting for transfers between devices, body(): lax.psum_scatter(part_num, 'group', scatter_dimension=0, tiled=True)  36.5 us
    dot_general x4, matrix products, body(): jnp.einsum('sr,sf->rf', chooser, block_out.reshape(slot_rows, HQ * HD), p...  17.7 us
    all_gather x1, blocking collectives, body(): by_groups = lax.all_gather(queries, 'group', axis=0, tiled=True)  16.1 us
    unnamed x37, local copies, waits for them, and re-layouts  12.5 us
  transfers between devices with their start and end apart: 4, of which 4 were waited for; matrix products, arithmetic and copies ran while one was open for 3% of the time, Pallas kernels for 0%

commit v1 on v0

v1 whole, which is shorter than its diff:
```python
import functools
import math

import jax
import jax.numpy as jnp
from jax import lax
from jax.experimental import pallas as pl
from jax.experimental.pallas import tpu as pltpu
from jax.sharding import PartitionSpec as P

HD = 128
DOCS = 4
TOKD = 128
ROWS = 128
R_GROUP = 16
NEAR = 8
LABELS = 32
STAT = 8
PIECE = 2 * R_GROUP + STAT
SCALE = 1.0 / math.sqrt(HD)
AXES = ("owner", "group")


def flat(y, z, x, core):
    return (((y % 4) * 2 + (z % 8) // 4) * 4 + x % 4) * 8 + (z % 4) * 2 + core


def chips():
    return [(y, z, x, c) for y in range(4) for z in range(8) for x in range(4) for c in range(2)]


def home(y, zh, x, group):
    return flat(y, 4 * zh + group - 2, x, zh)


def to_home():
    return [
        (flat(y, z, x, c), home(y, z // 4, x, (z % 4) * 2 + c)) for y, z, x, c in chips()
    ]


def home_groups():
    return [
        [home(y, zh, x, group) for x in range(4) for group in range(8)]
        for y in range(4)
        for zh in range(2)
    ]


def head_to(step, cross):
    return [(flat(y, z, x, c), flat(y + step, z, x, c ^ cross)) for y, z, x, c in chips()]


PIECES = [(step, cross) for step in range(4) for cross in range(2)]


def pack_body(keys, values, *rest):
    outs, sems = rest[:NEAR], rest[NEAR]
    owner, group = lax.axis_index("owner"), lax.axis_index("group")
    y, core = owner // 8, group % 2
    copies = []
    for place, (step, cross) in enumerate(PIECES):
        other = core if cross == 0 else 1 - core
        head = ((y + step) % 4) * 2 + other
        lanes = pl.ds(pl.multiple_of(head * HD, HD), HD)
        copies.append(
            pltpu.make_async_copy(keys.at[:, :, lanes], outs[place].at[0], sems.at[2 * place])
        )
        copies.append(
            pltpu.make_async_copy(
                values.at[:, :, lanes], outs[place].at[1], sems.at[2 * place + 1]
            )
        )
    for copy in copies:
        copy.start()
    for copy in copies:
        copy.wait()


def pack(keys, values):
    shape = jax.ShapeDtypeStruct((2, DOCS, TOKD, HD), keys.dtype)
    return pl.pallas_call(
        pack_body,
        out_shape=[shape] * NEAR,
        in_specs=[pl.BlockSpec(memory_space=pl.ANY)] * 2,
        out_specs=[pl.BlockSpec(memory_space=pl.ANY)] * NEAR,
        scratch_shapes=[pltpu.SemaphoreType.DMA((2 * NEAR,))],
        name="pack_heads",
    )(keys, values)


def attend_body(docs, queries, *rest):
    pieces, out = rest[:NEAR], rest[NEAR]
    doc = jnp.concatenate([docs[...]] * 2, axis=0)
    hot = jnp.concatenate(
        [
            jnp.broadcast_to((doc == d).astype(jnp.float32), (2 * ROWS, HD)).astype(jnp.bfloat16)
            for d in range(DOCS)
        ],
        axis=1,
    )
    lane = lax.broadcasted_iota(jnp.int32, (ROWS, HD), 1)

    def heads(pair, carry):
        both = queries[pl.ds(pair * ROWS, ROWS), :]
        rows = jnp.concatenate([both[:, :HD], both[:, HD:]], axis=0)
        wide = jnp.concatenate([rows] * DOCS, axis=1) * hot
        scores, tops = [], []
        for first in range(0, NEAR, 2):
            stretch = jnp.concatenate(
                [
                    jnp.concatenate([pieces[n][0, d] for d in range(DOCS)], axis=1)
                    for n in (first, first + 1)
                ],
                axis=0,
            )
            found = lax.dot_general(
                wide, stretch, (((1,), (1,)), ((), ())), preferred_element_type=jnp.float32
            )
            for half in (found[:, :TOKD], found[:, TOKD:]):
                scores.append(half)
                tops.append(jnp.max(half, axis=1, keepdims=True))
        top = functools.reduce(jnp.maximum, tops)
        numer = jnp.zeros((2 * ROWS, HD), jnp.float32)
        spread = jnp.zeros((2 * ROWS, TOKD), jnp.float32)
        for n in range(NEAR):
            expo = jnp.exp((scores[n] - tops[n]) * SCALE)
            factor = jnp.exp((tops[n] - top) * SCALE)
            weights = jnp.concatenate([expo.astype(jnp.bfloat16)] * DOCS, axis=1) * hot
            part = jnp.dot(
                weights,
                pieces[n][1].reshape(DOCS * TOKD, HD),
                preferred_element_type=jnp.float32,
            )
            numer = numer + part * factor
            spread = spread + expo * factor
        total = jnp.sum(spread, axis=1, keepdims=True)
        columns = jnp.where(
            lane == 0,
            top[:ROWS],
            jnp.where(
                lane == 1, top[ROWS:], jnp.where(lane == 2, total[:ROWS], total[ROWS:])
            ),
        )
        stats = columns.T[:STAT]
        for group in range(8):
            place = pair * 8 + group
            at = group * R_GROUP
            out[place, 0:R_GROUP, :] = numer[at : at + R_GROUP]
            out[place, R_GROUP : 2 * R_GROUP, :] = numer[ROWS + at : ROWS + at + R_GROUP]
            out[place, 2 * R_GROUP : PIECE, :] = stats
        return carry

    lax.fori_loop(0, 4, heads, 0)


def attend(req_doc, queries, pieces):
    return pl.pallas_call(
        attend_body,
        out_shape=jax.ShapeDtypeStruct((LABELS, PIECE, HD), jnp.float32),
        in_specs=[pl.BlockSpec(memory_space=pltpu.VMEM)] * (2 + NEAR),
        out_specs=pl.BlockSpec(memory_space=pltpu.VMEM),
        compiler_params=pltpu.CompilerParams(vmem_limit_bytes=40 * 1024 * 1024),
        name="attend_blocks",
    )(req_doc, queries, *pieces)


def merge_body(parts, out, shares):
    group = (lax.axis_index("owner") // 4 % 2) * 4 + lax.axis_index("group") // 2
    core = lax.axis_index("group") % 2
    group = (group + 2 - 4 * core + 8) % 8
    for half in range(2):
        tops = parts[:, 2 * R_GROUP + half, :]
        sums = parts[:, 2 * R_GROUP + 2 + half, :]
        top = jnp.max(tops, axis=0, keepdims=True)
        factor = jnp.exp((tops - top) * SCALE)
        share = factor / jnp.sum(factor * sums, axis=0, keepdims=True)
        padded = jnp.concatenate(
            [share, jnp.zeros((ROWS - LABELS, ROWS), jnp.float32)], axis=0
        )
        shares[...] = padded.T
        mine = shares[pl.ds(pl.multiple_of(group * R_GROUP, R_GROUP), R_GROUP), :]
        rows = slice(half * R_GROUP, (half + 1) * R_GROUP)
        acc = jnp.zeros((R_GROUP, HD), jnp.float32)
        for source in range(LABELS):
            acc = acc + mine[:, source : source + 1] * parts[source, rows, :]
        out[:, half * HD : (half + 1) * HD] = acc.astype(jnp.bfloat16)


def merge(parts):
    return pl.pallas_call(
        merge_body,
        out_shape=jax.ShapeDtypeStruct((R_GROUP, 2 * HD), jnp.bfloat16),
        in_specs=[pl.BlockSpec(memory_space=pltpu.VMEM)],
        out_specs=pl.BlockSpec(memory_space=pltpu.VMEM),
        scratch_shapes=[pltpu.VMEM((ROWS, ROWS), jnp.float32)],
        name="merge_parts",
    )(parts)


def body(queries, keys, values, req_doc):
    there = to_home()
    back = [(b, a) for a, b in there]
    groups = home_groups()
    moved = lax.ppermute(queries, AXES, there)
    own = pack(keys, values)
    pieces = [own[0]] + [
        lax.ppermute(own[n], AXES, head_to(*PIECES[n])) for n in range(1, NEAR)
    ]
    spread = jnp.broadcast_to(moved[None], (LABELS,) + moved.shape)
    gathered = lax.all_to_all(spread, AXES, 0, 0, axis_index_groups=groups, tiled=True)
    parts = attend(req_doc, gathered.reshape(LABELS * R_GROUP, 2 * HD), pieces)
    parts = lax.all_to_all(parts, AXES, 0, 0, axis_index_groups=groups, tiled=True)
    return lax.ppermute(merge(parts), AXES, back)


def solution(mesh):
    placed = (
        P("group", "owner"),
        P(None, ("owner", "group"), None),
        P(None, ("owner", "group"), None),
        P(),
    )
    return jax.shard_map(
        body, mesh=mesh, in_specs=placed, out_specs=P("group", "owner"), check_vma=False
    )
```

time: 554 us -> 157 us (0.28)
  blocking collectives: 291 us -> 27.4 us
  waiting for transfers between devices: 178 us -> 29.6 us
  Pallas kernels: 0 us -> 72.2 us
  matrix products: 37.4 us -> 0 us
  starting transfers between devices: 0.13 us -> 26.2 us
  local copies, waits for them, and re-layouts: 22.2 us -> 1.46 us
  between operations: 14.1 us -> 0.07 us
  other arithmetic: 10.6 us -> 0 us
    unnamed x1 -> x0, blocking collectives: 202 us -> none
    all_gather x1 -> x0, waiting for transfers between devices: 91.4 us -> none  [body(): gathered = lax.all_gather(by_groups, 'owner', axis=1, tiled=True)]
    reduce_scatter x3 -> x0, waiting for transfers between devices: 86.8 us -> none  [the longest x1 46.9 us: body(): lax.psum_scatter(part_den, 'group', scatter_dimension=0, tiled=True)]
    pmax x1 -> x0, blocking collectives: 72.6 us -> none  [body(): lax.pmax(maxima.astype(jnp.bfloat16), ('owner', 'group'))]
    pallas_call x0 -> x3, Pallas kernels: none -> 72.2 us  [the longest x1 64.8 us: pack(): pl.pallas_call(pack_body, out_shape=[shape] * NEAR, in_specs=[pl.BlockSpe...]
    dot_general x21 -> x0, matrix products: 37.4 us -> none  [the longest x4 17.7 us: body(): jnp.einsum('sr,sf->rf', chooser, block_out.reshape(slot_rows, HQ * HD), p...]
    ppermute x0 -> x9, waiting for transfers between devices: none -> 29.6 us  [the longest x7 22.4 us: body(): lax.ppermute(own[n], AXES, head_to(*PIECES[n]))]
    all_to_all x0 -> x1, blocking collectives: none -> 27.4 us  [body(): lax.all_to_all(parts, AXES, 0, 0, axis_index_groups=groups, tiled=True)]
  transfers between devices with their start and end apart: 4 -> 10, of which waited for: 4 -> 7; matrix products, arithmetic and copies ran while one was open for 3% -> 1% of each run, Pallas kernels for 0% -> 0%
where the time goes in v1:
time: 157 us
  Pallas kernels  72.2 us (46%)
  waiting for transfers between devices  29.6 us (19%)
  blocking collectives  27.4 us (17%)
  starting transfers between devices  26.2 us (17%)
    pallas_call x1, Pallas kernels, pack(): pl.pallas_call(pack_body, out_shape=[shape] * NEAR, in_specs=[pl.BlockSpe...  64.8 us
    all_to_all x1, blocking collectives, body(): lax.all_to_all(parts, AXES, 0, 0, axis_index_groups=groups, tiled=True)  27.4 us
    ppermute x7, waiting for transfers between devices, body(): lax.ppermute(own[n], AXES, head_to(*PIECES[n]))  22.4 us
    all_to_all x1, starting transfers between devices, body(): lax.all_to_all(spread, AXES, 0, 0, axis_index_groups=groups, tiled=True)  8.98 us
    ppermute x1, starting transfers between devices, body(): moved = lax.ppermute(queries, AXES, there)  8.2 us
    ppermute x7, starting transfers between devices, body(): lax.ppermute(own[n], AXES, head_to(*PIECES[n]))  7.08 us
    ppermute x1, waiting for transfers between devices, body(): return lax.ppermute(merge(parts), AXES, back)  5.94 us
    pallas_call x1, Pallas kernels, attend(): pl.pallas_call(attend_body, out_shape=jax.ShapeDtypeStruct((LABELS, PIECE...  5.29 us
  transfers between devices with their start and end apart: 10, of which 7 were waited for; matrix products, arithmetic and copies ran while one was open for 1% of the time, Pallas kernels for 0%

profile of v1, /device:TPU:8, one launch (start us, length us, event | category | flops | bytes accessed | tf_op | source)
XLA Modules:
  0.0 156.9 jit_solution(7203914936747357274)
XLA Ops:
  0.0 64.8 %pack_heads.1 = (bf16[2,4,128,128]{3,2,1,0:T(8,128)(2,1)}, bf16[2,4,128,128]{3,2,1,0:T(8,128)(2,1)}, bf16[2,4,128,128]{3,2,1,0:T(8,128)(2,1)}, bf16[2,4,128,128]...) custom-call(bf16[4,128,1024]{2,1,0:T(8,128)(2,1)} %keys.1, ...), custom_call_target="tpu_custom_call" | custom-call | tf_op jit(solution)/shard_map/pack_heads/pallas_call | solution.py:82
  64.8 0.1 collective-permute-start.1
  64.9 1.7 %collective-permute-start.2 = (bf16[2,4,128,128]{3,2,1,0:T(8,128)(2,1)}, bf16[2,4,128,128]{3,2,1,0:T(8,128)(2,1)S(1)}, u32[]{:S(2)}, u32[]{:S(2)}) collective-permute-start(bf16[2,4,128,128]{3,2,1,0:T(8,128)(2,1)} %get-tuple-element.15), channel_id=1, source_target_pairs={{0,64},{1,65},{8,72},{9,73},{16,80},{17,81},{24,88},{25,89},{2,66}... | collective-permute-start | bytes 786440 | tf_op jit(solution)/shard_map/ppermute | solution.py:208
  66.5 8.2 %collective-permute-start = (bf16[16,256]{1,0:T(8,128)(2,1)S(1)}, bf16[16,256]{1,0:T(8,128)(2,1)S(1)}, u32[]{:S(2)}, u32[]{:S(2)}) collective-permute-start(bf16[16,256]{1,0:T(8,128)(2,1)S(1)} %copy-done.4), channel_id=1, source_target_pairs={{0,36},{1,38},{8,44},{9,46},{16,52},{17,54},{24,60},{25,62},{2,0},... | collective-permute-start | bytes 24584 | tf_op jit(solution)/shard_map/ppermute | solution.py:205
  74.7 1.3 collective-permute-done
  76.1 0.7 broadcast_in_dim.2
  76.8 9.0 %all-to-all-start = ((bf16[32,16,256]{2,1,0:T(8,128)(2,1)}), bf16[32,16,256]{2,1,0:T(8,128)(2,1)S(1)}, u32[]{:S(2)}, u32[]{:S(2)}) async-start(bf16[32,16,256]{2,1,0:T(8,128)(2,1)} %broadcast_in_dim.2), calls=%async_computation | async-start | bytes 524288 | tf_op jit(solution)/shard_map/all_to_all | solution.py:211
  85.8 0.1 collective-permute-start.3
  85.9 1.0 collective-permute-start.4
  86.9 3.2 %collective-permute-start.5 = (bf16[2,4,128,128]{3,2,1,0:T(8,128)(2,1)}, bf16[2,4,128,128]{3,2,1,0:T(8,128)(2,1)S(1)}, u32[]{:S(2)}, u32[]{:S(2)}) collective-permute-start(bf16[2,4,128,128]{3,2,1,0:T(8,128)(2,1)} %get-tuple-element.18), channel_id=1, source_target_pairs={{0,129},{1,128},{8,137},{9,136},{16,145},{17,144},{24,153},{25,152... | collective-permute-start | bytes 786440 | tf_op jit(solution)/shard_map/ppermute | solution.py:208
  90.2 0.8 collective-permute-start.6
  91.0 0.2 collective-permute-start.7
  91.2 0.1 copy.5.docs
  91.3 3.4 %collective-permute-done.3.rest_3_ = bf16[2,4,128,128]{3,2,1,0:T(8,128)(2,1)S(1)} collective-permute-done((bf16[2,4,128,128]{3,2,1,0:T(8,128)(2,1)}, bf16[2,4,128,128]{3,2,1,0:T(8,128)(2,1)S(1)}, u32[]{:S(2)}, u32[]{:S(2)}) %collective-permute-start.3) | collective-permute-done | bytes 262176 | tf_op jit(solution)/shard_map/ppermute | solution.py:208
  94.7 2.0 %collective-permute-done.4.rest_4_ = bf16[2,4,128,128]{3,2,1,0:T(8,128)(2,1)S(1)} collective-permute-done((bf16[2,4,128,128]{3,2,1,0:T(8,128)(2,1)}, bf16[2,4,128,128]{3,2,1,0:T(8,128)(2,1)S(1)}, u32[]{:S(2)}, u32[]{:S(2)}) %collective-permute-start.4) | collective-permute-done | bytes 262176 | tf_op jit(solution)/shard_map/ppermute | solution.py:208
  96.7 6.2 %collective-permute-done.5.rest_5_ = bf16[2,4,128,128]{3,2,1,0:T(8,128)(2,1)S(1)} collective-permute-done((bf16[2,4,128,128]{3,2,1,0:T(8,128)(2,1)}, bf16[2,4,128,128]{3,2,1,0:T(8,128)(2,1)S(1)}, u32[]{:S(2)}, u32[]{:S(2)}) %collective-permute-start.5) | collective-permute-done | bytes 262176 | tf_op jit(solution)/shard_map/ppermute | solution.py:208
  102.9 5.3 %collective-permute-done.6.rest_6_ = bf16[2,4,128,128]{3,2,1,0:T(8,128)(2,1)S(1)} collective-permute-done((bf16[2,4,128,128]{3,2,1,0:T(8,128)(2,1)S(1)}, bf16[2,4,128,128]{3,2,1,0:T(8,128)(2,1)S(1)}, u32[]{:S(2)}, u32[]{:S(2)}) %collective-permute-start.6) | collective-permute-done | bytes 262176 | tf_op jit(solution)/shard_map/ppermute | solution.py:208
  108.2 5.4 %collective-permute-done.7.rest_7_ = bf16[2,4,128,128]{3,2,1,0:T(8,128)(2,1)S(1)} collective-permute-done((bf16[2,4,128,128]{3,2,1,0:T(8,128)(2,1)S(1)}, bf16[2,4,128,128]{3,2,1,0:T(8,128)(2,1)S(1)}, u32[]{:S(2)}, u32[]{:S(2)}) %collective-permute-start.7) | collective-permute-done | bytes 262176 | tf_op jit(solution)/shard_map/ppermute | solution.py:208
  113.6 5.3 %attend_blocks.1 = f32[32,40,128]{2,1,0:T(8,128)S(1)} custom-call(s32[128,1]{1,0:T(8,128)S(1)} %copy.5.docs, bf16[512,256]{1,0:T(8,128)(2,1)S(1)} %bitcast.1, bf16[2,4,128,128]{3,2,1,0:T(8,128)(2,1)S(1)} %copy-done, bf16[2,4,128,128]{3,2,1,0:T(8,128)(2,1)S(1)} %collective-permute-done.1.rest_1_, bf16[2,4,128,128]{3,2,1,0:T(8,128)(2,1)S(1)} %collective-permute-done.2.rest_2_, ...), custom_call_target="tpu_custom_call" | custom-call | tf_op jit(solution)/shard_map/attend_blocks/pallas_call | solution.py:158
  118.9 27.4 %all_to_all.10.parts = f32[32,40,128]{2,1,0:T(8,128)} all-to-all(f32[32,40,128]{2,1,0:T(8,128)S(1)} %attend_blocks.1), channel_id=1, replica_groups={{36,38,0,2,4,6,32,34,44,46,8,10,12,14,40,42,52,54,16,18,20,22,48,50,60,..., dimensions={0} | all-to-all | bytes 1310720 | tf_op jit(solution)/shard_map/all_to_all | solution.py:213
  146.3 2.2 %merge_parts.1 = bf16[16,256]{1,0:T(8,128)(2,1)} custom-call(f32[32,40,128]{2,1,0:T(8,128)} %all_to_all.10.parts), custom_call_target="tpu_custom_call" | custom-call | tf_op jit(solution)/shard_map/merge_parts/pallas_call | solution.py:191
  148.5 1.9 %collective-permute-start.8 = (bf16[16,256]{1,0:T(8,128)(2,1)}, bf16[16,256]{1,0:T(8,128)(2,1)S(1)}, u32[]{:S(2)}, u32[]{:S(2)}) collective-permute-start(bf16[16,256]{1,0:T(8,128)(2,1)} %merge_parts.1), channel_id=1, source_target_pairs={{36,0},{38,1},{44,8},{46,9},{52,16},{54,17},{60,24},{62,25},{0,2},... | collective-permute-start | bytes 24584 | tf_op jit(solution)/shard_map/ppermute | solution.py:214
  150.4 5.9 %collective-permute-done.8 = bf16[16,256]{1,0:T(8,128)(2,1)S(1)} collective-permute-done((bf16[16,256]{1,0:T(8,128)(2,1)}, bf16[16,256]{1,0:T(8,128)(2,1)S(1)}, u32[]{:S(2)}, u32[]{:S(2)}) %collective-permute-start.8) | collective-permute-done | bytes 8224 | tf_op jit(solution)/shard_map/ppermute | solution.py:214
  156.3 0.6 copy.7
  (13 shorter events, 0.0 us)
Async XLA Ops:
  0.0 66.5 %copy-start.4 = (bf16[16,256]{1,0:T(8,128)(2,1)S(1)}, bf16[16,256]{1,0:T(8,128)(2,1)}, u32[]{:S(2)}) copy-start(bf16[16,256]{1,0:T(8,128)(2,1)} %param.4) | copy-start | bytes 24580
  64.8 25.4 %collective-permute-start.1 = (bf16[2,4,128,128]{3,2,1,0:T(8,128)(2,1)}, bf16[2,4,128,128]{3,2,1,0:T(8,128)(2,1)S(1)}, u32[]{:S(2)}, u32[]{:S(2)}) collective-permute-start(bf16[2,4,128,128]{3,2,1,0:T(8,128)(2,1)} %get-tuple-element.14), channel_id=1, source_target_pairs={{0,1},{1,0},{8,9},{9,8},{16,17},{17,16},{24,25},{25,24},{2,3},{3,2... | collective-permute-start | bytes 786440 | tf_op jit(solution)/shard_map/ppermute | solution.py:208
  64.9 26.1 %collective-permute-start.2 = (bf16[2,4,128,128]{3,2,1,0:T(8,128)(2,1)}, bf16[2,4,128,128]{3,2,1,0:T(8,128)(2,1)S(1)}, u32[]{:S(2)}, u32[]{:S(2)}) collective-permute-start(bf16[2,4,128,128]{3,2,1,0:T(8,128)(2,1)} %get-tuple-element.15), channel_id=1, source_target_pairs={{0,64},{1,65},{8,72},{9,73},{16,80},{17,81},{24,88},{25,89},{2,66}... | collective-permute-start | bytes 786440 | tf_op jit(solution)/shard_map/ppermute | solution.py:208
  66.5 9.5 %collective-permute-start = (bf16[16,256]{1,0:T(8,128)(2,1)S(1)}, bf16[16,256]{1,0:T(8,128)(2,1)S(1)}, u32[]{:S(2)}, u32[]{:S(2)}) collective-permute-start(bf16[16,256]{1,0:T(8,128)(2,1)S(1)} %copy-done.4), channel_id=1, source_target_pairs={{0,36},{1,38},{8,44},{9,46},{16,52},{17,54},{24,60},{25,62},{2,0},... | collective-permute-start | bytes 24584 | tf_op jit(solution)/shard_map/ppermute | solution.py:205
  76.1 14.1 %copy-start.3 = (bf16[2,4,128,128]{3,2,1,0:T(8,128)(2,1)S(1)}, bf16[2,4,128,128]{3,2,1,0:T(8,128)(2,1)}, u32[]{:S(2)}) copy-start(bf16[2,4,128,128]{3,2,1,0:T(8,128)(2,1)} %get-tuple-element.19) | copy-start | bytes 786436
  76.8 14.2 %copy-start.2 = (bf16[2,4,128,128]{3,2,1,0:T(8,128)(2,1)S(1)}, bf16[2,4,128,128]{3,2,1,0:T(8,128)(2,1)}, u32[]{:S(2)}) copy-start(bf16[2,4,128,128]{3,2,1,0:T(8,128)(2,1)} %get-tuple-element.20) | copy-start | bytes 786436
  76.8 36.8 %copy-start = (bf16[2,4,128,128]{3,2,1,0:T(8,128)(2,1)S(1)}, bf16[2,4,128,128]{3,2,1,0:T(8,128)(2,1)}, u32[]{:S(2)}) copy-start(bf16[2,4,128,128]{3,2,1,0:T(8,128)(2,1)} %get-tuple-element.13.rest_0_) | copy-start | bytes 786436
  76.8 36.8 %all-to-all-start = ((bf16[32,16,256]{2,1,0:T(8,128)(2,1)}), bf16[32,16,256]{2,1,0:T(8,128)(2,1)S(1)}, u32[]{:S(2)}, u32[]{:S(2)}) async-start(bf16[32,16,256]{2,1,0:T(8,128)(2,1)} %broadcast_in_dim.2), calls=%async_computation | async-start | bytes 524288 | tf_op jit(solution)/shard_map/all_to_all | solution.py:211
  85.8 8.9 %collective-permute-start.3 = (bf16[2,4,128,128]{3,2,1,0:T(8,128)(2,1)}, bf16[2,4,128,128]{3,2,1,0:T(8,128)(2,1)S(1)}, u32[]{:S(2)}, u32[]{:S(2)}) collective-permute-start(bf16[2,4,128,128]{3,2,1,0:T(8,128)(2,1)} %get-tuple-element.16), channel_id=1, source_target_pairs={{0,65},{1,64},{8,73},{9,72},{16,81},{17,80},{24,89},{25,88},{2,67}... | collective-permute-start | bytes 786440 | tf_op jit(solution)/shard_map/ppermute | solution.py:208
  85.9 10.8 %collective-permute-start.4 = (bf16[2,4,128,128]{3,2,1,0:T(8,128)(2,1)}, bf16[2,4,128,128]{3,2,1,0:T(8,128)(2,1)S(1)}, u32[]{:S(2)}, u32[]{:S(2)}) collective-permute-start(bf16[2,4,128,128]{3,2,1,0:T(8,128)(2,1)} %get-tuple-element.17), channel_id=1, source_target_pairs={{0,128},{1,129},{8,136},{9,137},{16,144},{17,145},{24,152},{25,153... | collective-permute-start | bytes 786440 | tf_op jit(solution)/shard_map/ppermute | solution.py:208
  86.9 15.9 %collective-permute-start.5 = (bf16[2,4,128,128]{3,2,1,0:T(8,128)(2,1)}, bf16[2,4,128,128]{3,2,1,0:T(8,128)(2,1)S(1)}, u32[]{:S(2)}, u32[]{:S(2)}) collective-permute-start(bf16[2,4,128,128]{3,2,1,0:T(8,128)(2,1)} %get-tuple-element.18), channel_id=1, source_target_pairs={{0,129},{1,128},{8,137},{9,136},{16,145},{17,144},{24,153},{25,152... | collective-permute-start | bytes 786440 | tf_op jit(solution)/shard_map/ppermute | solution.py:208
  90.2 1.0 copy-start.1
  90.2 18.1 %collective-permute-start.6 = (bf16[2,4,128,128]{3,2,1,0:T(8,128)(2,1)S(1)}, bf16[2,4,128,128]{3,2,1,0:T(8,128)(2,1)S(1)}, u32[]{:S(2)}, u32[]{:S(2)}) collective-permute-start(bf16[2,4,128,128]{3,2,1,0:T(8,128)(2,1)S(1)} %copy-done.3), channel_id=1, source_target_pairs={{0,192},{1,193},{8,200},{9,201},{16,208},{17,209},{24,216},{25,217... | collective-permute-start | bytes 786440 | tf_op jit(solution)/shard_map/ppermute | solution.py:208
  91.0 22.7 %collective-permute-start.7 = (bf16[2,4,128,128]{3,2,1,0:T(8,128)(2,1)S(1)}, bf16[2,4,128,128]{3,2,1,0:T(8,128)(2,1)S(1)}, u32[]{:S(2)}, u32[]{:S(2)}) collective-permute-start(bf16[2,4,128,128]{3,2,1,0:T(8,128)(2,1)S(1)} %copy-done.2), channel_id=1, source_target_pairs={{0,193},{1,192},{8,201},{9,200},{16,209},{17,208},{24,217},{25,216... | collective-permute-start | bytes 786440 | tf_op jit(solution)/shard_map/ppermute | solution.py:208
  148.5 7.9 %collective-permute-start.8 = (bf16[16,256]{1,0:T(8,128)(2,1)}, bf16[16,256]{1,0:T(8,128)(2,1)S(1)}, u32[]{:S(2)}, u32[]{:S(2)}) collective-permute-start(bf16[16,256]{1,0:T(8,128)(2,1)} %merge_parts.1), channel_id=1, source_target_pairs={{36,0},{38,1},{44,8},{46,9},{52,16},{54,17},{60,24},{62,25},{0,2},... | collective-permute-start | bytes 24584 | tf_op jit(solution)/shard_map/ppermute | solution.py:214

commit v2 on v0

v2 whole, which is shorter than its diff:
```python
import functools
import math

import jax
import jax.numpy as jnp
from jax import lax
from jax.experimental import pallas as pl
from jax.experimental.pallas import tpu as pltpu
from jax.sharding import PartitionSpec as P

HD = 128
DOCS = 4
TOKD = 128
ROWS = 128
R_GROUP = 16
NEAR = 8
LABELS = 32
HALF = 64
FIRST = 1 << 20
FIRST_UNROLL = 1
LAST_UNROLL = 4
ORDER = 1 << 34
STAT = 8
EARLY = 6
FINE = HALF - 3
PIECE = 3 * R_GROUP
BOX = 4 * DOCS * TOKD
SCALE = math.log2(math.e) / math.sqrt(HD)
AXES = ("owner", "group")


def flat(y, z, x, core):
    return (((y % 4) * 2 + (z % 8) // 4) * 4 + x % 4) * 8 + (z % 4) * 2 + core


def chips():
    return [(y, z, x, c) for y in range(4) for z in range(8) for x in range(4) for c in range(2)]


def planes():
    return [
        [flat(y, 4 * zh + zl, x, c) for zh in range(2) for x in range(4) for zl in range(4)]
        for y in range(4)
        for c in range(2)
    ]


def along_y(step):
    return [(flat(y, z, x, c), flat(y + step, z, x, c)) for y, z, x, c in chips()]


def other_core():
    return [(flat(y, z, x, c), flat(y, z, x, 1 - c)) for y, z, x, c in chips()]


def span(head, kind, doc):
    first = ((head * 2 + kind) * DOCS + doc) * TOKD
    return slice(first, first + TOKD)


def pack_body(keys, values, queries, docs, *rest):
    boxes, spread = rest[:4], rest[4]
    held, asked, names, sems = rest[5:]
    y = lax.axis_index("owner") // 8
    copies = [
        pltpu.make_async_copy(source.at[doc], held.at[kind, doc], sems.at[kind, doc])
        for doc in range(DOCS)
        for kind, source in enumerate((keys, values))
    ]
    copies.append(pltpu.make_async_copy(queries, asked, sems.at[2, 0]))
    copies.append(pltpu.make_async_copy(docs, names, sems.at[2, 1]))
    for copy in copies:
        copy.start()
    for n, copy in enumerate(copies[: 2 * DOCS]):
        copy.wait()
        doc, kind = n // 2, n % 2
        for step in range(4):
            for head in range(2):
                lanes = pl.ds(pl.multiple_of((((y + step) % 4) * 2 + head) * HD, HD), HD)
                boxes[step][span(head, kind, doc), :] = held[kind, doc, :, lanes]
    copies[2 * DOCS].wait()
    spread[...] = jnp.broadcast_to(asked[...][None], spread.shape)
    copies[2 * DOCS + 1].wait()
    row = names[...].astype(jnp.float32)
    boxes[0][BOX:, :] = jnp.broadcast_to(row, (R_GROUP, ROWS)).astype(jnp.bfloat16)


def pack(keys, values, queries, docs):
    kept = [
        pltpu.with_memory_space_constraint(x, pltpu.HBM) for x in (keys, values, queries, docs)
    ]
    return pl.pallas_call(
        pack_body,
        out_shape=[
            jax.ShapeDtypeStruct((BOX + extra, HD), keys.dtype) for extra in (R_GROUP, 0, 0, 0)
        ]
        + [jax.ShapeDtypeStruct((LABELS,) + queries.shape, queries.dtype)],
        in_specs=[pl.BlockSpec(memory_space=pltpu.HBM)] * 4,
        out_specs=[pl.BlockSpec(memory_space=pltpu.VMEM)] * 5,
        scratch_shapes=[
            pltpu.VMEM((2,) + keys.shape, keys.dtype),
            pltpu.VMEM(queries.shape, queries.dtype),
            pltpu.VMEM(docs.shape, docs.dtype),
            pltpu.SemaphoreType.DMA((3, DOCS)),
        ],
        compiler_params=pltpu.CompilerParams(vmem_limit_bytes=12 * 1024 * 1024),
        name="pack_heads",
    )(*kept)


def doc_mask(home, column):
    core = lax.axis_index("group") % 2
    docs = home[BOX : BOX + 1, :].astype(jnp.float32)
    column[...] = jnp.broadcast_to(docs, (ROWS, ROWS)).T
    names = [
        column[pl.ds(pl.multiple_of((2 * zl + core) * R_GROUP, R_GROUP), R_GROUP), :]
        for zl in range(4)
    ]
    doc = jnp.concatenate(names * 4, axis=0)
    return jnp.concatenate(
        [(doc == d).astype(jnp.float32).astype(jnp.bfloat16) for d in range(DOCS)], axis=1
    )


def order_body(queries, out):
    for turn in range(4):
        for half in range(2):
            rows = queries[turn * ROWS : (turn + 1) * ROWS, half * HD : (half + 1) * HD]
            out[turn, half * ROWS : (half + 1) * ROWS, :] = rows


def order(queries):
    return pl.pallas_call(
        order_body,
        out_shape=jax.ShapeDtypeStruct((4, 2 * ROWS, HD), queries.dtype),
        in_specs=[pl.BlockSpec(memory_space=pltpu.VMEM)],
        out_specs=pl.BlockSpec(memory_space=pltpu.VMEM),
        cost_estimate=pl.CostEstimate(flops=ORDER, bytes_accessed=1 << 19, transcendentals=0),
        compiler_params=pltpu.CompilerParams(vmem_limit_bytes=4 * 1024 * 1024),
        name="order_queries",
    )(queries)


def find_scores(turn, queries, boxes, hot):
    wide = jnp.concatenate([queries[turn]] * DOCS, axis=1) * hot
    scores, tops = [], []
    for left in range(0, len(boxes), 2):
        stretch = jnp.concatenate(
            [
                jnp.concatenate(
                    [part(box, turn, d * TOKD, TOKD) for d in range(DOCS)], axis=1
                )
                for box in boxes[left : left + 2]
            ],
            axis=0,
        )
        found = lax.dot_general(
            wide, stretch, (((1,), (1,)), ((), ())), preferred_element_type=jnp.float32
        )
        for one in (found[:, :TOKD], found[:, TOKD:]):
            scores.append(one)
            tops.append(jnp.max(one, axis=1, keepdims=True))
    return scores, tops


def part(box, turn, start, size):
    first = (turn // 2) * (BOX // 2)
    return box[pl.ds(pl.multiple_of(first + start, TOKD), size), :]


def add_values(turn, boxes, hot, scores, tops, top, numer):
    spread = jnp.zeros((2 * ROWS, TOKD), jnp.float32)
    for box, score, own in zip(boxes, scores, tops):
        expo = jnp.exp2((score - own) * SCALE)
        factor = jnp.exp2((own - top) * SCALE)
        weights = jnp.concatenate([expo.astype(jnp.bfloat16)] * DOCS, axis=1) * hot
        summed = jnp.dot(
            weights,
            part(box, turn, DOCS * TOKD, DOCS * TOKD),
            preferred_element_type=jnp.float32,
        )
        numer = numer + summed * factor
        spread = spread + expo * factor
    return numer, jnp.sum(spread, axis=1, keepdims=True)


def first_body(queries, *rest):
    boxes, numer_out, stat_out, column = rest[:EARLY], *rest[EARLY:]
    hot = doc_mask(boxes[0], column)
    lane = lax.broadcasted_iota(jnp.int32, (ROWS, HD), 1)

    def heads(turn, carry):
        scores, tops = find_scores(turn, queries, boxes, hot)
        top = functools.reduce(jnp.maximum, tops)
        numer, total = add_values(
            turn, boxes, hot, scores, tops, top, jnp.zeros((2 * ROWS, HD), jnp.float32)
        )
        numer_out[turn] = numer
        columns = jnp.zeros((ROWS, HD), jnp.float32)
        for place, value in enumerate((top[:ROWS], top[ROWS:], total[:ROWS], total[ROWS:])):
            columns = jnp.where(lane == place, value, columns)
        stat_out[turn] = columns.T[:STAT]
        return carry

    lax.fori_loop(0, 4, heads, 0, unroll=FIRST_UNROLL)


def attend_first(queries, boxes):
    return pl.pallas_call(
        first_body,
        out_shape=[
            jax.ShapeDtypeStruct((4, 2 * ROWS, HD), jnp.float32),
            jax.ShapeDtypeStruct((4, STAT, ROWS), jnp.float32),
        ],
        in_specs=[pl.BlockSpec(memory_space=pltpu.VMEM)] * (1 + EARLY),
        out_specs=[pl.BlockSpec(memory_space=pltpu.VMEM)] * 2,
        scratch_shapes=[pltpu.VMEM((ROWS, ROWS), jnp.float32)],
        cost_estimate=pl.CostEstimate(flops=FIRST, bytes_accessed=4 << 20, transcendentals=0),
        compiler_params=pltpu.CompilerParams(vmem_limit_bytes=16 * 1024 * 1024),
        name="attend_first",
    )(queries, *boxes)


def last_body(queries, numer_in, stat_in, home, *rest):
    boxes, out, column = rest[: NEAR - EARLY], *rest[NEAR - EARLY :]
    hot = doc_mask(home, column)
    lane = lax.broadcasted_iota(jnp.int32, (ROWS, HD), 1)

    def heads(turn, carry):
        scores, tops = find_scores(turn, queries, boxes, hot)
        padded = jnp.concatenate(
            [stat_in[turn], jnp.zeros((ROWS - STAT, ROWS), jnp.float32)], axis=0
        ).T
        old_top = jnp.concatenate([padded[:, 0:1], padded[:, 1:2]], axis=0)
        old_total = jnp.concatenate([padded[:, 2:3], padded[:, 3:4]], axis=0)
        top = functools.reduce(jnp.maximum, [old_top] + tops)
        top = top.astype(jnp.bfloat16).astype(jnp.float32)
        factor = jnp.exp2((old_top - top) * SCALE)
        numer, total = add_values(
            turn, boxes, hot, scores, tops, top, numer_in[turn] * factor
        )
        total = total + old_total * factor
        high = numer.astype(jnp.bfloat16)
        low = numer - high.astype(jnp.float32)
        total_high = total.astype(jnp.bfloat16).astype(jnp.float32)
        total_low = total - total_high
        extra = jnp.where(lane < HALF, low[:ROWS], low[ROWS:])
        for half in range(2):
            at = slice(half * ROWS, (half + 1) * ROWS)
            for place, value in enumerate((top, total_high, total_low)):
                extra = jnp.where(lane == half * HALF + FINE + place, value[at], extra)
        extra = extra.astype(jnp.bfloat16)
        for n in range(8):
            at = n * R_GROUP
            place = turn * 8 + n
            out[place, 0:R_GROUP, :] = high[at : at + R_GROUP]
            out[place, R_GROUP : 2 * R_GROUP, :] = high[ROWS + at : ROWS + at + R_GROUP]
            out[place, 2 * R_GROUP :, :] = extra[at : at + R_GROUP]
        return carry

    lax.fori_loop(0, 4, heads, 0, unroll=LAST_UNROLL)


def attend_last(queries, state, home, boxes):
    return pl.pallas_call(
        last_body,
        out_shape=jax.ShapeDtypeStruct((LABELS, PIECE, HD), jnp.bfloat16),
        in_specs=[pl.BlockSpec(memory_space=pltpu.VMEM)] * (4 + NEAR - EARLY),
        out_specs=pl.BlockSpec(memory_space=pltpu.VMEM),
        scratch_shapes=[pltpu.VMEM((ROWS, ROWS), jnp.float32)],
        compiler_params=pltpu.CompilerParams(vmem_limit_bytes=16 * 1024 * 1024),
        name="attend_last",
    )(queries, *state, home, *boxes)


def merge_body(parts, out):
    lane = lax.broadcasted_iota(jnp.int32, (R_GROUP, HD), 1)
    extras = [parts[n, 2 * R_GROUP :, :].astype(jnp.float32) for n in range(LABELS)]
    top = functools.reduce(jnp.maximum, extras)
    numer = [jnp.zeros((R_GROUP, HD), jnp.float32) for _ in range(2)]
    rest = [jnp.zeros((R_GROUP, HD), jnp.float32) for _ in range(2)]
    for n in range(LABELS):
        factors = jnp.exp2((extras[n] - top) * SCALE)
        for half in range(2):
            at = half * HALF + FINE
            factor = factors[:, at : at + 1]
            high = parts[n, half * R_GROUP : (half + 1) * R_GROUP, :].astype(jnp.float32)
            numer[half] = numer[half] + factor * high
            rest[half] = rest[half] + factor * extras[n]
    for half in range(2):
        first = half * HALF
        fine = (lane >= first) & (lane < first + FINE)
        whole = numer[half] + jnp.where(fine, rest[half], 0.0)
        sums = rest[half][:, first + FINE + 1 : first + FINE + 3]
        total = sums[:, 0:1] + sums[:, 1:2]
        out[:, half * HD : (half + 1) * HD] = (whole / total).astype(jnp.bfloat16)


def merge(parts):
    return pl.pallas_call(
        merge_body,
        out_shape=jax.ShapeDtypeStruct((R_GROUP, 2 * HD), jnp.bfloat16),
        in_specs=[pl.BlockSpec(memory_space=pltpu.VMEM)],
        out_specs=pl.BlockSpec(memory_space=pltpu.VMEM),
        name="merge_parts",
    )(parts)


def body(queries, keys, values, req_doc):
    groups = planes()
    home, *boxes, spread = pack(keys, values, queries, req_doc.reshape(1, ROWS))
    up, opposite, down = boxes
    up, down = (lax.ppermute(box, AXES, along_y(step)) for box, step in ((up, 1), (down, 3)))
    opposite, up, down = lax.optimization_barrier((opposite, up, down))
    opposite = lax.ppermute(opposite, AXES, along_y(2))
    pairs = [(box, lax.ppermute(box, AXES, other_core())) for box in (home, up, down)]
    gathered = lax.all_to_all(spread, AXES, 0, 0, axis_index_groups=groups, tiled=True)
    gathered = order(gathered.reshape(LABELS * R_GROUP, 2 * HD))
    state = attend_first(gathered, sum(pairs, ()))
    state, opposite = lax.optimization_barrier((state, opposite))
    last = (opposite, lax.ppermute(opposite, AXES, other_core()))
    parts = attend_last(gathered, state, home, last)
    parts = lax.all_to_all(parts, AXES, 0, 0, axis_index_groups=groups, tiled=True)
    return merge(parts)


def solution(mesh):
    placed = (
        P("group", "owner"),
        P(None, ("owner", "group"), None),
        P(None, ("owner", "group"), None),
        P(),
    )
    return jax.shard_map(
        body, mesh=mesh, in_specs=placed, out_specs=P("group", "owner"), check_vma=False
    )
```

time: 554 us -> 66.5 us (0.12)
  blocking collectives: 291 us -> 24.4 us
  waiting for transfers between devices: 178 us -> 12 us
  matrix products: 37.4 us -> 0 us
  local copies, waits for them, and re-layouts: 22.2 us -> 0 us
  starting transfers between devices: 0.13 us -> 16.4 us
  between operations: 14.1 us -> 0.08 us
  Pallas kernels: 0 us -> 13.1 us
  other arithmetic: 10.6 us -> 0 us
    unnamed x1 -> x0, blocking collectives: 202 us -> none
    all_gather x1 -> x0, waiting for transfers between devices: 91.4 us -> none  [body(): gathered = lax.all_gather(by_groups, 'owner', axis=1, tiled=True)]
    reduce_scatter x3 -> x0, waiting for transfers between devices: 86.8 us -> none  [the longest x1 46.9 us: body(): lax.psum_scatter(part_den, 'group', scatter_dimension=0, tiled=True)]
    pmax x1 -> x0, blocking collectives: 72.6 us -> none  [body(): lax.pmax(maxima.astype(jnp.bfloat16), ('owner', 'group'))]
    dot_general x21 -> x0, matrix products: 37.4 us -> none  [the longest x4 17.7 us: body(): jnp.einsum('sr,sf->rf', chooser, block_out.reshape(slot_rows, HQ * HD), p...]
    all_to_all x0 -> x1, blocking collectives: none -> 24.4 us  [body(): lax.all_to_all(parts, AXES, 0, 0, axis_index_groups=groups, tiled=True)]
    all_gather x1 -> x0, blocking collectives: 16.1 us -> none  [body(): by_groups = lax.all_gather(queries, 'group', axis=0, tiled=True)]
    pallas_call x0 -> x5, Pallas kernels: none -> 13.1 us  [the longest x1 5.77 us: attend_first(): pl.pallas_call(first_body, out_shape=[jax.ShapeDtypeStruct((4, 2 * ROWS,...]
  transfers between devices with their start and end apart: 4 -> 8, of which waited for: 4 -> 4; matrix products, arithmetic and copies ran while one was open for 3% -> 0% of each run, Pallas kernels for 0% -> 9%
where the time goes in v2:
time: 66.5 us; the launch traced here: 66 us
  blocking collectives  24.4 us (37%)
  starting transfers between devices  16.4 us (25%)
  Pallas kernels  13.1 us (20%)
  waiting for transfers between devices  12 us (18%)
    all_to_all x1, blocking collectives, body(): lax.all_to_all(parts, AXES, 0, 0, axis_index_groups=groups, tiled=True)  24.4 us
    all_to_all x1, starting transfers between devices, body(): lax.all_to_all(spread, AXES, 0, 0, axis_index_groups=groups, tiled=True)  11.1 us
    all_to_all x1, waiting for transfers between devices, body(): lax.all_to_all(spread, AXES, 0, 0, axis_index_groups=groups, tiled=True)  8.61 us
    pallas_call x1, Pallas kernels, attend_first(): pl.pallas_call(first_body, out_shape=[jax.ShapeDtypeStruct((4, 2 * ROWS,...  5.77 us
    pallas_call x1, Pallas kernels, attend_last(): pl.pallas_call(last_body, out_shape=jax.ShapeDtypeStruct((LABELS, PIECE,...  2.64 us
    pallas_call x1, Pallas kernels, pack(): pl.pallas_call(pack_body, out_shape=[jax.ShapeDtypeStruct((BOX + extra, H...  2.59 us
    ppermute x2, starting transfers between devices, body(): lax.ppermute(box, AXES, along_y(step))  2.35 us
    ppermute x1, starting transfers between devices, body(): opposite = lax.ppermute(opposite, AXES, along_y(2))  2.3 us
  transfers between devices with their start and end apart: 8, of which 4 were waited for; matrix products, arithmetic and copies ran while one was open for 0% of the time, Pallas kernels for 9%

profile of v2, /device:TPU:8, one launch (start us, length us, event | category | flops | bytes accessed | tf_op | source)
XLA Modules:
  0.0 66.0 jit_solution(12187480875148494909)
XLA Ops:
  0.0 2.6 %pack_heads.1 = (bf16[2064,128]{1,0:T(8,128)(2,1)S(1)}, bf16[2048,128]{1,0:T(8,128)(2,1)S(1)}, bf16[2048,128]{1,0:T(8,128)(2,1)}, bf16[2048,128]{1,0:T(8,128)(2,1)S(1)}, bf16[32,16,256]{2,1,0:T(8,128)(2,1)}) custom-call(bf16[4,128,1024]{2,1,0:T(8,128)(2,1)} %keys.1, bf16[4,128,1024]{2,1,0:T(8,128)(2,1)} %values.1, bf16[16,256]{1,0:T(8,128)(2,1)} %queries.1, ...), custom_call_target="tpu_custom_call" | custom-call | tf_op jit(solution)/shard_map/pack_heads/pallas_call | solution.py:92
  2.6 1.7 %collective-permute-start.1 = (bf16[2048,128]{1,0:T(8,128)(2,1)S(1)}, bf16[2048,128]{1,0:T(8,128)(2,1)S(1)}, u32[]{:S(2)}, u32[]{:S(2)}) collective-permute-start(bf16[2048,128]{1,0:T(8,128)(2,1)S(1)} %get-tuple-element.21), channel_id=1, source_target_pairs={{0,64},{1,65},{8,72},{9,73},{16,80},{17,81},{24,88},{25,89},{2,66}... | collective-permute-start | bytes 1572872 | tf_op jit(solution)/shard_map/ppermute | solution.py:313
  4.3 0.7 %collective-permute-start.2 = (bf16[2048,128]{1,0:T(8,128)(2,1)S(1)}, bf16[2048,128]{1,0:T(8,128)(2,1)S(1)}, u32[]{:S(2)}, u32[]{:S(2)}) collective-permute-start(bf16[2048,128]{1,0:T(8,128)(2,1)S(1)} %get-tuple-element.22), channel_id=1, source_target_pairs={{0,192},{1,193},{8,200},{9,201},{16,208},{17,209},{24,216},{25,217... | collective-permute-start | bytes 1572872 | tf_op jit(solution)/shard_map/ppermute | solution.py:313
  5.0 11.1 %all-to-all-start = ((bf16[32,16,256]{2,1,0:T(8,128)(2,1)}), bf16[32,16,256]{2,1,0:T(8,128)(2,1)S(1)}, u32[]{:S(2)}, u32[]{:S(2)}) async-start(bf16[32,16,256]{2,1,0:T(8,128)(2,1)} %get-tuple-element.18), calls=%async_computation | async-start | bytes 524288 | tf_op jit(solution)/shard_map/all_to_all | solution.py:317
  16.0 0.1 collective-permute-start
  16.1 0.2 collective-permute-done.1.rest_2_
  16.3 1.3 %collective-permute-done.2.rest_4_ = bf16[2048,128]{1,0:T(8,128)(2,1)S(1)} collective-permute-done((bf16[2048,128]{1,0:T(8,128)(2,1)S(1)}, bf16[2048,128]{1,0:T(8,128)(2,1)S(1)}, u32[]{:S(2)}, u32[]{:S(2)}) %collective-permute-start.2) | collective-permute-done | bytes 524320 | tf_op jit(solution)/shard_map/ppermute | solution.py:313
  17.6 2.3 %collective-permute-start.5 = (bf16[2048,128]{1,0:T(8,128)(2,1)}, bf16[2048,128]{1,0:T(8,128)(2,1)S(1)}, u32[]{:S(2)}, u32[]{:S(2)}) collective-permute-start(bf16[2048,128]{1,0:T(8,128)(2,1)} %get-tuple-element.27), channel_id=1, source_target_pairs={{0,128},{1,129},{8,136},{9,137},{16,144},{17,145},{24,152},{25,153... | collective-permute-start | bytes 1572872 | tf_op jit(solution)/shard_map/ppermute | solution.py:315
  19.9 0.0 collective-permute-start.3
  19.9 0.5 collective-permute-start.4
  20.4 8.6 %all-to-all-done = bf16[32,16,256]{2,1,0:T(8,128)(2,1)S(1)} async-done(((bf16[32,16,256]{2,1,0:T(8,128)(2,1)}), bf16[32,16,256]{2,1,0:T(8,128)(2,1)S(1)}, u32[]{:S(2)}, u32[]{:S(2)}) %all-to-all-start) | async-done | bytes 262176 | tf_op jit(solution)/shard_map/all_to_all | solution.py:317
  29.1 0.0 collective-permute-done.rest_1_
  29.1 0.0 collective-permute-done.3.rest_3_
  29.1 0.0 collective-permute-done.4.rest_5_
  29.1 5.8 %attend_first.1 = (f32[4,256,128]{2,1,0:T(8,128)S(1)}, f32[4,8,128]{2,1,0:T(8,128)S(1)}) custom-call(bf16[4,256,128]{2,1,0:T(8,128)(2,1)S(1)} %order_queries.1.queries, bf16[2064,128]{1,0:T(8,128)(2,1)S(1)} %get-tuple-element.19.rest_0_.home, bf16[2064,128]{1,0:T(8,128)(2,1)S(1)} %collective-permute-done.rest_1_, ...), custom_call_target="tpu_custom_call" | custom-call | flops 1048576 | bytes 4194304 | tf_op jit(solution)/shard_map/attend_first/pallas_call | solution.py:209
  34.9 0.0 collective-permute-done.5.rest_0_
  34.9 0.1 collective-permute-start.6
  35.0 1.9 %collective-permute-done.6.rest_1_ = bf16[2048,128]{1,0:T(8,128)(2,1)S(1)} collective-permute-done((bf16[2048,128]{1,0:T(8,128)(2,1)S(1)}, bf16[2048,128]{1,0:T(8,128)(2,1)S(1)}, u32[]{:S(2)}, u32[]{:S(2)}) %collective-permute-start.6) | collective-permute-done | bytes 524320 | tf_op jit(solution)/shard_map/ppermute | solution.py:321
  36.9 2.6 %attend_last.1 = bf16[32,48,128]{2,1,0:T(8,128)(2,1)S(1)} custom-call(bf16[4,256,128]{2,1,0:T(8,128)(2,1)S(1)} %order_queries.1.queries, f32[4,256,128]{2,1,0:T(8,128)S(1)} %get-tuple-element.28.numer_in, f32[4,8,128]{2,1,0:T(8,128)S(1)} %get-tuple-element.29.stat_in, bf16[2064,128]{1,0:T(8,128)(2,1)S(1)} %get-tuple-element.19.rest_0_.home, ...), custom_call_target="tpu_custom_call" | custom-call | tf_op jit(solution)/shard_map/attend_last/pallas_call | solution.py:265
  39.6 24.4 %all_to_all.10.parts = bf16[32,48,128]{2,1,0:T(8,128)(2,1)} all-to-all(bf16[32,48,128]{2,1,0:T(8,128)(2,1)S(1)} %attend_last.1), channel_id=1, replica_groups={{0,2,4,6,8,10,12,14,16,18,20,22,24,26,28,30,32,34,36,38,40,42,44,46,48,..., dimensions={0} | all-to-all | bytes 786432 | tf_op jit(solution)/shard_map/all_to_all | solution.py:323
  63.9 2.0 %merge_parts.1 = bf16[16,256]{1,0:T(8,128)(2,1)} custom-call(bf16[32,48,128]{2,1,0:T(8,128)(2,1)} %all_to_all.10.parts), custom_call_target="tpu_custom_call" | custom-call | tf_op jit(solution)/shard_map/merge_parts/pallas_call | solution.py:300
  (1 shorter events, 0.0 us)
Async XLA Ops:
  2.6 13.7 %collective-permute-start.1 = (bf16[2048,128]{1,0:T(8,128)(2,1)S(1)}, bf16[2048,128]{1,0:T(8,128)(2,1)S(1)}, u32[]{:S(2)}, u32[]{:S(2)}) collective-permute-start(bf16[2048,128]{1,0:T(8,128)(2,1)S(1)} %get-tuple-element.21), channel_id=1, source_target_pairs={{0,64},{1,65},{8,72},{9,73},{16,80},{17,81},{24,88},{25,89},{2,66}... | collective-permute-start | bytes 1572872 | tf_op jit(solution)/shard_map/ppermute | solution.py:313
  4.3 13.4 %collective-permute-start.2 = (bf16[2048,128]{1,0:T(8,128)(2,1)S(1)}, bf16[2048,128]{1,0:T(8,128)(2,1)S(1)}, u32[]{:S(2)}, u32[]{:S(2)}) collective-permute-start(bf16[2048,128]{1,0:T(8,128)(2,1)S(1)} %get-tuple-element.22), channel_id=1, source_target_pairs={{0,192},{1,193},{8,200},{9,201},{16,208},{17,209},{24,216},{25,217... | collective-permute-start | bytes 1572872 | tf_op jit(solution)/shard_map/ppermute | solution.py:313
  5.0 24.1 %all-to-all-start = ((bf16[32,16,256]{2,1,0:T(8,128)(2,1)}), bf16[32,16,256]{2,1,0:T(8,128)(2,1)S(1)}, u32[]{:S(2)}, u32[]{:S(2)}) async-start(bf16[32,16,256]{2,1,0:T(8,128)(2,1)} %get-tuple-element.18), calls=%async_computation | async-start | bytes 524288 | tf_op jit(solution)/shard_map/all_to_all | solution.py:317
  16.0 13.1 %collective-permute-start = (bf16[2064,128]{1,0:T(8,128)(2,1)S(1)}, bf16[2064,128]{1,0:T(8,128)(2,1)S(1)}, u32[]{:S(2)}, u32[]{:S(2)}) collective-permute-start(bf16[2064,128]{1,0:T(8,128)(2,1)S(1)} %get-tuple-element.19.rest_0_.home), channel_id=1, source_target_pairs={{0,1},{1,0},{8,9},{9,8},{16,17},{17,16},{24,25},{25,24},{2,3},{3,2... | collective-permute-start | bytes 1585160 | tf_op jit(solution)/shard_map/ppermute | solution.py:316
  17.6 17.3 %collective-permute-start.5 = (bf16[2048,128]{1,0:T(8,128)(2,1)}, bf16[2048,128]{1,0:T(8,128)(2,1)S(1)}, u32[]{:S(2)}, u32[]{:S(2)}) collective-permute-start(bf16[2048,128]{1,0:T(8,128)(2,1)} %get-tuple-element.27), channel_id=1, source_target_pairs={{0,128},{1,129},{8,136},{9,137},{16,144},{17,145},{24,152},{25,153... | collective-permute-start | bytes 1572872 | tf_op jit(solution)/shard_map/ppermute | solution.py:315
  19.9 9.2 %collective-permute-start.3 = (bf16[2048,128]{1,0:T(8,128)(2,1)S(1)}, bf16[2048,128]{1,0:T(8,128)(2,1)S(1)}, u32[]{:S(2)}, u32[]{:S(2)}) collective-permute-start(bf16[2048,128]{1,0:T(8,128)(2,1)S(1)} %collective-permute-done.1.rest_2_), channel_id=1, source_target_pairs={{0,1},{1,0},{8,9},{9,8},{16,17},{17,16},{24,25},{25,24},{2,3},{3,2... | collective-permute-start | bytes 1572872 | tf_op jit(solution)/shard_map/ppermute | solution.py:316
  19.9 9.2 %collective-permute-start.4 = (bf16[2048,128]{1,0:T(8,128)(2,1)S(1)}, bf16[2048,128]{1,0:T(8,128)(2,1)}, u32[]{:S(2)}, u32[]{:S(2)}) collective-permute-start(bf16[2048,128]{1,0:T(8,128)(2,1)S(1)} %collective-permute-done.2.rest_4_), channel_id=1, source_target_pairs={{0,1},{1,0},{8,9},{9,8},{16,17},{17,16},{24,25},{25,24},{2,3},{3,2... | collective-permute-start | bytes 1572872 | tf_op jit(solution)/shard_map/ppermute | solution.py:316
  34.9 2.0 %collective-permute-start.6 = (bf16[2048,128]{1,0:T(8,128)(2,1)S(1)}, bf16[2048,128]{1,0:T(8,128)(2,1)S(1)}, u32[]{:S(2)}, u32[]{:S(2)}) collective-permute-start(bf16[2048,128]{1,0:T(8,128)(2,1)S(1)} %collective-permute-done.5.rest_0_), channel_id=1, source_target_pairs={{0,1},{1,0},{8,9},{9,8},{16,17},{17,16},{24,25},{25,24},{2,3},{3,2... | collective-permute-start | bytes 1572872 | tf_op jit(solution)/shard_map/ppermute | solution.py:321

commit v3 on v2

--- a/solution.py
+++ b/solution.py
@@ -110,7 +110,7 @@
 
 def doc_mask(home, column):
     core = lax.axis_index("group") % 2
-    docs = home[BOX : BOX + 1, :].astype(jnp.float32)
+    docs = home[BOX:, :].astype(jnp.float32)[:1]
     column[...] = jnp.broadcast_to(docs, (ROWS, ROWS)).T
     names = [
         column[pl.ds(pl.multiple_of((2 * zl + core) * R_GROUP, R_GROUP), R_GROUP), :]
@@ -303,7 +303,7 @@
         in_specs=[pl.BlockSpec(memory_space=pltpu.VMEM)],
         out_specs=pl.BlockSpec(memory_space=pltpu.VMEM),
         name="merge_parts",
-    )(parts)
+    )(pltpu.with_memory_space_constraint(parts, pltpu.VMEM))
 
 
 def body(queries, keys, values, req_doc):
@@ -311,7 +311,7 @@
     home, *boxes, spread = pack(keys, values, queries, req_doc.reshape(1, ROWS))
     up, opposite, down = boxes
     up, down = (lax.ppermute(box, AXES, along_y(step)) for box, step in ((up, 1), (down, 3)))
-    opposite, up, down = lax.optimization_barrier((opposite, up, down))
+    opposite, up = lax.optimization_barrier((opposite, up))
     opposite = lax.ppermute(opposite, AXES, along_y(2))
     pairs = [(box, lax.ppermute(box, AXES, other_core())) for box in (home, up, down)]
     gathered = lax.all_to_all(spread, AXES, 0, 0, axis_index_groups=groups, tiled=True)

time: 66.5 us -> 65.2 us (0.980)
  blocking collectives: 24.4 us -> 23.3 us
  Pallas kernels: 13.1 us -> 12.3 us
    all_to_all x1, waiting for transfers between devices: 8.61 us -> 9.91 us  [body(): lax.all_to_all(spread, AXES, 0, 0, axis_index_groups=groups, tiled=True)]
    ppermute x2, waiting for transfers between devices: 1.51 us -> 0.21 us  [body(): lax.ppermute(box, AXES, along_y(step))]
    all_to_all x1, blocking collectives: 24.4 us -> 23.3 us  [body(): lax.all_to_all(parts, AXES, 0, 0, axis_index_groups=groups, tiled=True)]
    pallas_call x1, Pallas kernels: 2.04 us -> 1.05 us  [merge(): pl.pallas_call(merge_body, out_shape=jax.ShapeDtypeStruct((R_GROUP, 2 * H...]
  transfers between devices with their start and end apart: 8 -> 8, of which waited for: 4 -> 3; matrix products, arithmetic and copies ran while one was open for 0% -> 0% of each run, Pallas kernels for 9% -> 9%
where the time goes in v3:
time: 65.2 us; the launch traced here: 64.1 us
  blocking collectives  23.3 us (36%)
  starting transfers between devices  16.4 us (25%)
  Pallas kernels  12.3 us (19%)
  waiting for transfers between devices  12 us (18%)
    all_to_all x1, blocking collectives, body(): lax.all_to_all(parts, AXES, 0, 0, axis_index_groups=groups, tiled=True)  23.3 us
    all_to_all x1, starting transfers between devices, body(): lax.all_to_all(spread, AXES, 0, 0, axis_index_groups=groups, tiled=True)  11.1 us
    all_to_all x1, waiting for transfers between devices, body(): lax.all_to_all(spread, AXES, 0, 0, axis_index_groups=groups, tiled=True)  9.91 us
    pallas_call x1, Pallas kernels, attend_first(): pl.pallas_call(first_body, out_shape=[jax.ShapeDtypeStruct((4, 2 * ROWS,...  5.77 us
    pallas_call x1, Pallas kernels, pack(): pl.pallas_call(pack_body, out_shape=[jax.ShapeDtypeStruct((BOX + extra, H...  2.77 us
    pallas_call x1, Pallas kernels, attend_last(): pl.pallas_call(last_body, out_shape=jax.ShapeDtypeStruct((LABELS, PIECE,...  2.64 us
    ppermute x2, starting transfers between devices, body(): lax.ppermute(box, AXES, along_y(step))  2.35 us
    ppermute x1, starting transfers between devices, body(): opposite = lax.ppermute(opposite, AXES, along_y(2))  2.3 us
  transfers between devices with their start and end apart: 8, of which 3 were waited for; matrix products, arithmetic and copies ran while one was open for 0% of the time, Pallas kernels for 9%

profile of v3, /device:TPU:8, one launch (start us, length us, event | category | flops | bytes accessed | tf_op | source)
XLA Modules:
  0.0 64.1 jit_solution(3083965118149708024)
XLA Ops:
  0.0 2.8 %pack_heads.1 = (bf16[2064,128]{1,0:T(8,128)(2,1)S(1)}, bf16[2048,128]{1,0:T(8,128)(2,1)S(1)}, bf16[2048,128]{1,0:T(8,128)(2,1)}, bf16[2048,128]{1,0:T(8,128)(2,1)}, bf16[32,16,256]{2,1,0:T(8,128)(2,1)}) custom-call(bf16[4,128,1024]{2,1,0:T(8,128)(2,1)} %keys.1, bf16[4,128,1024]{2,1,0:T(8,128)(2,1)} %values.1, bf16[16,256]{1,0:T(8,128)(2,1)} %queries.1, ...), custom_call_target="tpu_custom_call" | custom-call | tf_op jit(solution)/shard_map/pack_heads/pallas_call | solution.py:92
  2.8 1.7 %collective-permute-start.1 = (bf16[2048,128]{1,0:T(8,128)(2,1)S(1)}, bf16[2048,128]{1,0:T(8,128)(2,1)S(1)}, u32[]{:S(2)}, u32[]{:S(2)}) collective-permute-start(bf16[2048,128]{1,0:T(8,128)(2,1)S(1)} %get-tuple-element.20), channel_id=1, source_target_pairs={{0,64},{1,65},{8,72},{9,73},{16,80},{17,81},{24,88},{25,89},{2,66}... | collective-permute-start | bytes 1572872 | tf_op jit(solution)/shard_map/ppermute | solution.py:313
  4.4 0.7 %collective-permute-start.3 = (bf16[2048,128]{1,0:T(8,128)(2,1)}, bf16[2048,128]{1,0:T(8,128)(2,1)S(1)}, u32[]{:S(2)}, u32[]{:S(2)}) collective-permute-start(bf16[2048,128]{1,0:T(8,128)(2,1)} %get-tuple-element.22), channel_id=1, source_target_pairs={{0,192},{1,193},{8,200},{9,201},{16,208},{17,209},{24,216},{25,217... | collective-permute-start | bytes 1572872 | tf_op jit(solution)/shard_map/ppermute | solution.py:313
  5.1 11.1 %all-to-all-start = ((bf16[32,16,256]{2,1,0:T(8,128)(2,1)}), bf16[32,16,256]{2,1,0:T(8,128)(2,1)S(1)}, u32[]{:S(2)}, u32[]{:S(2)}) async-start(bf16[32,16,256]{2,1,0:T(8,128)(2,1)} %get-tuple-element.17), calls=%async_computation | async-start | bytes 524288 | tf_op jit(solution)/shard_map/all_to_all | solution.py:317
  16.2 0.1 collective-permute-start
  16.3 0.2 collective-permute-done.1.rest_2_
  16.5 2.3 %collective-permute-start.5 = (bf16[2048,128]{1,0:T(8,128)(2,1)}, bf16[2048,128]{1,0:T(8,128)(2,1)S(1)}, u32[]{:S(2)}, u32[]{:S(2)}) collective-permute-start(bf16[2048,128]{1,0:T(8,128)(2,1)} %get-tuple-element.25), channel_id=1, source_target_pairs={{0,128},{1,129},{8,136},{9,137},{16,144},{17,145},{24,152},{25,153... | collective-permute-start | bytes 1572872 | tf_op jit(solution)/shard_map/ppermute | solution.py:315
  18.8 0.0 collective-permute-start.2
  18.8 0.0 collective-permute-done.3.rest_4_
  18.8 0.5 collective-permute-start.4
  19.3 9.9 %all-to-all-done = bf16[32,16,256]{2,1,0:T(8,128)(2,1)S(1)} async-done(((bf16[32,16,256]{2,1,0:T(8,128)(2,1)}), bf16[32,16,256]{2,1,0:T(8,128)(2,1)S(1)}, u32[]{:S(2)}, u32[]{:S(2)}) %all-to-all-start) | async-done | bytes 262176 | tf_op jit(solution)/shard_map/all_to_all | solution.py:317
  29.3 0.0 collective-permute-done.rest_1_
  29.3 0.0 collective-permute-done.2.rest_3_
  29.3 0.0 collective-permute-done.4.rest_5_
  29.3 5.8 %attend_first.1 = (f32[4,256,128]{2,1,0:T(8,128)S(1)}, f32[4,8,128]{2,1,0:T(8,128)S(1)}) custom-call(bf16[4,256,128]{2,1,0:T(8,128)(2,1)S(1)} %order_queries.1.queries, bf16[2064,128]{1,0:T(8,128)(2,1)S(1)} %get-tuple-element.18.rest_0_.home, bf16[2064,128]{1,0:T(8,128)(2,1)S(1)} %collective-permute-done.rest_1_, ...), custom_call_target="tpu_custom_call" | custom-call | flops 1048576 | bytes 4194304 | tf_op jit(solution)/shard_map/attend_first/pallas_call | solution.py:209
  35.1 0.0 collective-permute-done.5.rest_0_
  35.1 0.1 collective-permute-start.6
  35.2 1.9 %collective-permute-done.6.rest_1_ = bf16[2048,128]{1,0:T(8,128)(2,1)S(1)} collective-permute-done((bf16[2048,128]{1,0:T(8,128)(2,1)S(1)}, bf16[2048,128]{1,0:T(8,128)(2,1)S(1)}, u32[]{:S(2)}, u32[]{:S(2)}) %collective-permute-start.6) | collective-permute-done | bytes 524320 | tf_op jit(solution)/shard_map/ppermute | solution.py:321
  37.1 2.6 %attend_last.1 = bf16[32,48,128]{2,1,0:T(8,128)(2,1)S(1)} custom-call(bf16[4,256,128]{2,1,0:T(8,128)(2,1)S(1)} %order_queries.1.queries, f32[4,256,128]{2,1,0:T(8,128)S(1)} %get-tuple-element.26.numer_in, f32[4,8,128]{2,1,0:T(8,128)S(1)} %get-tuple-element.27.stat_in, bf16[2064,128]{1,0:T(8,128)(2,1)S(1)} %get-tuple-element.18.rest_0_.home, ...), custom_call_target="tpu_custom_call" | custom-call | tf_op jit(solution)/shard_map/attend_last/pallas_call | solution.py:265
  39.7 23.3 %all_to_all.10.parts = bf16[32,48,128]{2,1,0:T(8,128)(2,1)S(1)} all-to-all(bf16[32,48,128]{2,1,0:T(8,128)(2,1)S(1)} %attend_last.1), channel_id=1, replica_groups={{0,2,4,6,8,10,12,14,16,18,20,22,24,26,28,30,32,34,36,38,40,42,44,46,48,..., dimensions={0} | all-to-all | bytes 786432 | tf_op jit(solution)/shard_map/all_to_all | solution.py:323
  63.0 1.1 %merge_parts.1 = bf16[16,256]{1,0:T(8,128)(2,1)} custom-call(bf16[32,48,128]{2,1,0:T(8,128)(2,1)S(1)} %all_to_all.10.parts), custom_call_target="tpu_custom_call" | custom-call | tf_op jit(solution)/shard_map/merge_parts/pallas_call | solution.py:300
  (1 shorter events, 0.0 us)
Async XLA Ops:
  2.8 13.7 %collective-permute-start.1 = (bf16[2048,128]{1,0:T(8,128)(2,1)S(1)}, bf16[2048,128]{1,0:T(8,128)(2,1)S(1)}, u32[]{:S(2)}, u32[]{:S(2)}) collective-permute-start(bf16[2048,128]{1,0:T(8,128)(2,1)S(1)} %get-tuple-element.20), channel_id=1, source_target_pairs={{0,64},{1,65},{8,72},{9,73},{16,80},{17,81},{24,88},{25,89},{2,66}... | collective-permute-start | bytes 1572872 | tf_op jit(solution)/shard_map/ppermute | solution.py:313
  4.4 14.4 %collective-permute-start.3 = (bf16[2048,128]{1,0:T(8,128)(2,1)}, bf16[2048,128]{1,0:T(8,128)(2,1)S(1)}, u32[]{:S(2)}, u32[]{:S(2)}) collective-permute-start(bf16[2048,128]{1,0:T(8,128)(2,1)} %get-tuple-element.22), channel_id=1, source_target_pairs={{0,192},{1,193},{8,200},{9,201},{16,208},{17,209},{24,216},{25,217... | collective-permute-start | bytes 1572872 | tf_op jit(solution)/shard_map/ppermute | solution.py:313
  5.1 24.1 %all-to-all-start = ((bf16[32,16,256]{2,1,0:T(8,128)(2,1)}), bf16[32,16,256]{2,1,0:T(8,128)(2,1)S(1)}, u32[]{:S(2)}, u32[]{:S(2)}) async-start(bf16[32,16,256]{2,1,0:T(8,128)(2,1)} %get-tuple-element.17), calls=%async_computation | async-start | bytes 524288 | tf_op jit(solution)/shard_map/all_to_all | solution.py:317
  16.2 13.1 %collective-permute-start = (bf16[2064,128]{1,0:T(8,128)(2,1)S(1)}, bf16[2064,128]{1,0:T(8,128)(2,1)S(1)}, u32[]{:S(2)}, u32[]{:S(2)}) collective-permute-start(bf16[2064,128]{1,0:T(8,128)(2,1)S(1)} %get-tuple-element.18.rest_0_.home), channel_id=1, source_target_pairs={{0,1},{1,0},{8,9},{9,8},{16,17},{17,16},{24,25},{25,24},{2,3},{3,2... | collective-permute-start | bytes 1585160 | tf_op jit(solution)/shard_map/ppermute | solution.py:316
  16.5 18.6 %collective-permute-start.5 = (bf16[2048,128]{1,0:T(8,128)(2,1)}, bf16[2048,128]{1,0:T(8,128)(2,1)S(1)}, u32[]{:S(2)}, u32[]{:S(2)}) collective-permute-start(bf16[2048,128]{1,0:T(8,128)(2,1)} %get-tuple-element.25), channel_id=1, source_target_pairs={{0,128},{1,129},{8,136},{9,137},{16,144},{17,145},{24,152},{25,153... | collective-permute-start | bytes 1572872 | tf_op jit(solution)/shard_map/ppermute | solution.py:315
  18.8 10.5 %collective-permute-start.2 = (bf16[2048,128]{1,0:T(8,128)(2,1)S(1)}, bf16[2048,128]{1,0:T(8,128)(2,1)S(1)}, u32[]{:S(2)}, u32[]{:S(2)}) collective-permute-start(bf16[2048,128]{1,0:T(8,128)(2,1)S(1)} %collective-permute-done.1.rest_2_), channel_id=1, source_target_pairs={{0,1},{1,0},{8,9},{9,8},{16,17},{17,16},{24,25},{25,24},{2,3},{3,2... | collective-permute-start | bytes 1572872 | tf_op jit(solution)/shard_map/ppermute | solution.py:316
  18.8 10.5 %collective-permute-start.4 = (bf16[2048,128]{1,0:T(8,128)(2,1)S(1)}, bf16[2048,128]{1,0:T(8,128)(2,1)}, u32[]{:S(2)}, u32[]{:S(2)}) collective-permute-start(bf16[2048,128]{1,0:T(8,128)(2,1)S(1)} %collective-permute-done.3.rest_4_), channel_id=1, source_target_pairs={{0,1},{1,0},{8,9},{9,8},{16,17},{17,16},{24,25},{25,24},{2,3},{3,2... | collective-permute-start | bytes 1572872 | tf_op jit(solution)/shard_map/ppermute | solution.py:316
  35.1 2.0 %collective-permute-start.6 = (bf16[2048,128]{1,0:T(8,128)(2,1)S(1)}, bf16[2048,128]{1,0:T(8,128)(2,1)S(1)}, u32[]{:S(2)}, u32[]{:S(2)}) collective-permute-start(bf16[2048,128]{1,0:T(8,128)(2,1)S(1)} %collective-permute-done.5.rest_0_), channel_id=1, source_target_pairs={{0,1},{1,0},{8,9},{9,8},{16,17},{17,16},{24,25},{25,24},{2,3},{3,2... | collective-permute-start | bytes 1572872 | tf_op jit(solution)/shard_map/ppermute | solution.py:321

commit v4 on v3

--- a/solution.py
+++ b/solution.py
@@ -39,7 +39,7 @@
 
 def planes():
     return [
-        [flat(y, 4 * zh + zl, x, c) for zh in range(2) for x in range(4) for zl in range(4)]
+        [flat(y, 4 * zh + zl, x, c) for zl in range(4) for zh in range(2) for x in range(4)]
         for y in range(4)
         for c in range(2)
     ]
@@ -124,9 +124,12 @@
 
 def order_body(queries, out):
     for turn in range(4):
-        for half in range(2):
-            rows = queries[turn * ROWS : (turn + 1) * ROWS, half * HD : (half + 1) * HD]
-            out[turn, half * ROWS : (half + 1) * ROWS, :] = rows
+        for n in range(8):
+            place = (n % 4) * 8 + (turn // 2) * 4 + (turn % 2) * 2 + n // 4
+            block = queries[place * R_GROUP : (place + 1) * R_GROUP, :]
+            for half in range(2):
+                at = half * ROWS + n * R_GROUP
+                out[turn, at : at + R_GROUP, :] = block[:, half * HD : (half + 1) * HD]
 
 
 def order(queries):
@@ -252,7 +255,7 @@
         extra = extra.astype(jnp.bfloat16)
         for n in range(8):
             at = n * R_GROUP
-            place = turn * 8 + n
+            place = (n % 4) * 8 + (turn // 2) * 4 + (turn % 2) * 2 + n // 4
             out[place, 0:R_GROUP, :] = high[at : at + R_GROUP]
             out[place, R_GROUP : 2 * R_GROUP, :] = high[ROWS + at : ROWS + at + R_GROUP]
             out[place, 2 * R_GROUP :, :] = extra[at : at + R_GROUP]

time: 65.2 us -> 64.8 us (level)
  no operation moved by 1% of the time
where the time goes in v4:
time: 64.8 us; the launch traced here: 63.9 us
  blocking collectives  23.5 us (36%)
  starting transfers between devices  16.4 us (25%)
  Pallas kernels  12.3 us (19%)
  waiting for transfers between devices  11.6 us (18%)
    all_to_all x1, blocking collectives, body(): lax.all_to_all(parts, AXES, 0, 0, axis_index_groups=groups, tiled=True)  23.5 us
    all_to_all x1, starting transfers between devices, body(): lax.all_to_all(spread, AXES, 0, 0, axis_index_groups=groups, tiled=True)  11.1 us
    all_to_all x1, waiting for transfers between devices, body(): lax.all_to_all(spread, AXES, 0, 0, axis_index_groups=groups, tiled=True)  9.47 us
    pallas_call x1, Pallas kernels, attend_first(): pl.pallas_call(first_body, out_shape=[jax.ShapeDtypeStruct((4, 2 * ROWS,...  5.77 us
    pallas_call x1, Pallas kernels, pack(): pl.pallas_call(pack_body, out_shape=[jax.ShapeDtypeStruct((BOX + extra, H...  2.77 us
    pallas_call x1, Pallas kernels, attend_last(): pl.pallas_call(last_body, out_shape=jax.ShapeDtypeStruct((LABELS, PIECE,...  2.64 us
    ppermute x2, starting transfers between devices, body(): lax.ppermute(box, AXES, along_y(step))  2.35 us
    ppermute x1, starting transfers between devices, body(): opposite = lax.ppermute(opposite, AXES, along_y(2))  2.3 us
  transfers between devices with their start and end apart: 8, of which 3 were waited for; matrix products, arithmetic and copies ran while one was open for 0% of the time, Pallas kernels for 9%

profile of v4, /device:TPU:8, one launch (start us, length us, event | category | flops | bytes accessed | tf_op | source)
XLA Modules:
  0.0 63.9 jit_solution(1314587818694467107)
XLA Ops:
  0.0 2.8 %pack_heads.1 = (bf16[2064,128]{1,0:T(8,128)(2,1)S(1)}, bf16[2048,128]{1,0:T(8,128)(2,1)S(1)}, bf16[2048,128]{1,0:T(8,128)(2,1)}, bf16[2048,128]{1,0:T(8,128)(2,1)}, bf16[32,16,256]{2,1,0:T(8,128)(2,1)}) custom-call(bf16[4,128,1024]{2,1,0:T(8,128)(2,1)} %keys.1, bf16[4,128,1024]{2,1,0:T(8,128)(2,1)} %values.1, bf16[16,256]{1,0:T(8,128)(2,1)} %queries.1, ...), custom_call_target="tpu_custom_call" | custom-call | tf_op jit(solution)/shard_map/pack_heads/pallas_call | solution.py:92
  2.8 1.7 %collective-permute-start.1 = (bf16[2048,128]{1,0:T(8,128)(2,1)S(1)}, bf16[2048,128]{1,0:T(8,128)(2,1)S(1)}, u32[]{:S(2)}, u32[]{:S(2)}) collective-permute-start(bf16[2048,128]{1,0:T(8,128)(2,1)S(1)} %get-tuple-element.20), channel_id=1, source_target_pairs={{0,64},{1,65},{8,72},{9,73},{16,80},{17,81},{24,88},{25,89},{2,66}... | collective-permute-start | bytes 1572872 | tf_op jit(solution)/shard_map/ppermute | solution.py:316
  4.4 0.7 %collective-permute-start.3 = (bf16[2048,128]{1,0:T(8,128)(2,1)}, bf16[2048,128]{1,0:T(8,128)(2,1)S(1)}, u32[]{:S(2)}, u32[]{:S(2)}) collective-permute-start(bf16[2048,128]{1,0:T(8,128)(2,1)} %get-tuple-element.22), channel_id=1, source_target_pairs={{0,192},{1,193},{8,200},{9,201},{16,208},{17,209},{24,216},{25,217... | collective-permute-start | bytes 1572872 | tf_op jit(solution)/shard_map/ppermute | solution.py:316
  5.1 11.1 %all-to-all-start = ((bf16[32,16,256]{2,1,0:T(8,128)(2,1)}), bf16[32,16,256]{2,1,0:T(8,128)(2,1)S(1)}, u32[]{:S(2)}, u32[]{:S(2)}) async-start(bf16[32,16,256]{2,1,0:T(8,128)(2,1)} %get-tuple-element.17), calls=%async_computation | async-start | bytes 524288 | tf_op jit(solution)/shard_map/all_to_all | solution.py:320
  16.2 0.1 collective-permute-start
  16.3 0.2 collective-permute-done.1.rest_2_
  16.5 2.3 %collective-permute-start.5 = (bf16[2048,128]{1,0:T(8,128)(2,1)}, bf16[2048,128]{1,0:T(8,128)(2,1)S(1)}, u32[]{:S(2)}, u32[]{:S(2)}) collective-permute-start(bf16[2048,128]{1,0:T(8,128)(2,1)} %get-tuple-element.25), channel_id=1, source_target_pairs={{0,128},{1,129},{8,136},{9,137},{16,144},{17,145},{24,152},{25,153... | collective-permute-start | bytes 1572872 | tf_op jit(solution)/shard_map/ppermute | solution.py:318
  18.8 0.0 collective-permute-start.2
  18.8 0.0 collective-permute-done.3.rest_4_
  18.8 0.5 collective-permute-start.4
  19.3 9.5 %all-to-all-done = bf16[32,16,256]{2,1,0:T(8,128)(2,1)S(1)} async-done(((bf16[32,16,256]{2,1,0:T(8,128)(2,1)}), bf16[32,16,256]{2,1,0:T(8,128)(2,1)S(1)}, u32[]{:S(2)}, u32[]{:S(2)}) %all-to-all-start) | async-done | bytes 262176 | tf_op jit(solution)/shard_map/all_to_all | solution.py:320
  28.8 0.0 collective-permute-done.rest_1_
  28.8 0.0 collective-permute-done.2.rest_3_
  28.9 0.0 collective-permute-done.4.rest_5_
  28.9 5.8 %attend_first.1 = (f32[4,256,128]{2,1,0:T(8,128)S(1)}, f32[4,8,128]{2,1,0:T(8,128)S(1)}) custom-call(bf16[4,256,128]{2,1,0:T(8,128)(2,1)S(1)} %order_queries.1.queries, bf16[2064,128]{1,0:T(8,128)(2,1)S(1)} %get-tuple-element.18.rest_0_.home, bf16[2064,128]{1,0:T(8,128)(2,1)S(1)} %collective-permute-done.rest_1_, ...), custom_call_target="tpu_custom_call" | custom-call | flops 1048576 | bytes 4194304 | tf_op jit(solution)/shard_map/attend_first/pallas_call | solution.py:212
  34.6 0.0 collective-permute-done.5.rest_0_
  34.7 0.1 collective-permute-start.6
  34.8 1.9 %collective-permute-done.6.rest_1_ = bf16[2048,128]{1,0:T(8,128)(2,1)S(1)} collective-permute-done((bf16[2048,128]{1,0:T(8,128)(2,1)S(1)}, bf16[2048,128]{1,0:T(8,128)(2,1)S(1)}, u32[]{:S(2)}, u32[]{:S(2)}) %collective-permute-start.6) | collective-permute-done | bytes 524320 | tf_op jit(solution)/shard_map/ppermute | solution.py:324
  36.7 2.6 %attend_last.1 = bf16[32,48,128]{2,1,0:T(8,128)(2,1)S(1)} custom-call(bf16[4,256,128]{2,1,0:T(8,128)(2,1)S(1)} %order_queries.1.queries, f32[4,256,128]{2,1,0:T(8,128)S(1)} %get-tuple-element.26.numer_in, f32[4,8,128]{2,1,0:T(8,128)S(1)} %get-tuple-element.27.stat_in, bf16[2064,128]{1,0:T(8,128)(2,1)S(1)} %get-tuple-element.18.rest_0_.home, ...), custom_call_target="tpu_custom_call" | custom-call | tf_op jit(solution)/shard_map/attend_last/pallas_call | solution.py:268
  39.3 23.5 %all_to_all.10.parts = bf16[32,48,128]{2,1,0:T(8,128)(2,1)S(1)} all-to-all(bf16[32,48,128]{2,1,0:T(8,128)(2,1)S(1)} %attend_last.1), channel_id=1, replica_groups={{0,8,16,24,32,40,48,56,2,10,18,26,34,42,50,58,4,12,20,28,36,44,52,60,6,..., dimensions={0} | all-to-all | bytes 786432 | tf_op jit(solution)/shard_map/all_to_all | solution.py:326
  62.8 1.1 %merge_parts.1 = bf16[16,256]{1,0:T(8,128)(2,1)} custom-call(bf16[32,48,128]{2,1,0:T(8,128)(2,1)S(1)} %all_to_all.10.parts), custom_call_target="tpu_custom_call" | custom-call | tf_op jit(solution)/shard_map/merge_parts/pallas_call | solution.py:303
  (1 shorter events, 0.0 us)
Async XLA Ops:
  2.8 13.7 %collective-permute-start.1 = (bf16[2048,128]{1,0:T(8,128)(2,1)S(1)}, bf16[2048,128]{1,0:T(8,128)(2,1)S(1)}, u32[]{:S(2)}, u32[]{:S(2)}) collective-permute-start(bf16[2048,128]{1,0:T(8,128)(2,1)S(1)} %get-tuple-element.20), channel_id=1, source_target_pairs={{0,64},{1,65},{8,72},{9,73},{16,80},{17,81},{24,88},{25,89},{2,66}... | collective-permute-start | bytes 1572872 | tf_op jit(solution)/shard_map/ppermute | solution.py:316
  4.4 14.4 %collective-permute-start.3 = (bf16[2048,128]{1,0:T(8,128)(2,1)}, bf16[2048,128]{1,0:T(8,128)(2,1)S(1)}, u32[]{:S(2)}, u32[]{:S(2)}) collective-permute-start(bf16[2048,128]{1,0:T(8,128)(2,1)} %get-tuple-element.22), channel_id=1, source_target_pairs={{0,192},{1,193},{8,200},{9,201},{16,208},{17,209},{24,216},{25,217... | collective-permute-start | bytes 1572872 | tf_op jit(solution)/shard_map/ppermute | solution.py:316
  5.1 23.7 %all-to-all-start = ((bf16[32,16,256]{2,1,0:T(8,128)(2,1)}), bf16[32,16,256]{2,1,0:T(8,128)(2,1)S(1)}, u32[]{:S(2)}, u32[]{:S(2)}) async-start(bf16[32,16,256]{2,1,0:T(8,128)(2,1)} %get-tuple-element.17), calls=%async_computation | async-start | bytes 524288 | tf_op jit(solution)/shard_map/all_to_all | solution.py:320
  16.2 12.6 %collective-permute-start = (bf16[2064,128]{1,0:T(8,128)(2,1)S(1)}, bf16[2064,128]{1,0:T(8,128)(2,1)S(1)}, u32[]{:S(2)}, u32[]{:S(2)}) collective-permute-start(bf16[2064,128]{1,0:T(8,128)(2,1)S(1)} %get-tuple-element.18.rest_0_.home), channel_id=1, source_target_pairs={{0,1},{1,0},{8,9},{9,8},{16,17},{17,16},{24,25},{25,24},{2,3},{3,2... | collective-permute-start | bytes 1585160 | tf_op jit(solution)/shard_map/ppermute | solution.py:319
  16.5 18.1 %collective-permute-start.5 = (bf16[2048,128]{1,0:T(8,128)(2,1)}, bf16[2048,128]{1,0:T(8,128)(2,1)S(1)}, u32[]{:S(2)}, u32[]{:S(2)}) collective-permute-start(bf16[2048,128]{1,0:T(8,128)(2,1)} %get-tuple-element.25), channel_id=1, source_target_pairs={{0,128},{1,129},{8,136},{9,137},{16,144},{17,145},{24,152},{25,153... | collective-permute-start | bytes 1572872 | tf_op jit(solution)/shard_map/ppermute | solution.py:318
  18.8 10.0 %collective-permute-start.2 = (bf16[2048,128]{1,0:T(8,128)(2,1)S(1)}, bf16[2048,128]{1,0:T(8,128)(2,1)S(1)}, u32[]{:S(2)}, u32[]{:S(2)}) collective-permute-start(bf16[2048,128]{1,0:T(8,128)(2,1)S(1)} %collective-permute-done.1.rest_2_), channel_id=1, source_target_pairs={{0,1},{1,0},{8,9},{9,8},{16,17},{17,16},{24,25},{25,24},{2,3},{3,2... | collective-permute-start | bytes 1572872 | tf_op jit(solution)/shard_map/ppermute | solution.py:319
  18.8 10.0 %collective-permute-start.4 = (bf16[2048,128]{1,0:T(8,128)(2,1)S(1)}, bf16[2048,128]{1,0:T(8,128)(2,1)}, u32[]{:S(2)}, u32[]{:S(2)}) collective-permute-start(bf16[2048,128]{1,0:T(8,128)(2,1)S(1)} %collective-permute-done.3.rest_4_), channel_id=1, source_target_pairs={{0,1},{1,0},{8,9},{9,8},{16,17},{17,16},{24,25},{25,24},{2,3},{3,2... | collective-permute-start | bytes 1572872 | tf_op jit(solution)/shard_map/ppermute | solution.py:319
  34.7 2.0 %collective-permute-start.6 = (bf16[2048,128]{1,0:T(8,128)(2,1)S(1)}, bf16[2048,128]{1,0:T(8,128)(2,1)S(1)}, u32[]{:S(2)}, u32[]{:S(2)}) collective-permute-start(bf16[2048,128]{1,0:T(8,128)(2,1)S(1)} %collective-permute-done.5.rest_0_), channel_id=1, source_target_pairs={{0,1},{1,0},{8,9},{9,8},{16,17},{17,16},{24,25},{25,24},{2,3},{3,2... | collective-permute-start | bytes 1572872 | tf_op jit(solution)/shard_map/ppermute | solution.py:324
